TPU v7x, 512 devices: a whole 4x8x8 slice. The times are simulated.
512 devices in a mesh: dp: 64 (over y, x, core), expert: 8 (over z).
Axes of the slice: x: 4, y: 8, z: 8, core: 2. Of those that a mesh axis runs over, the one named last changes fastest.
Arguments:
- att_input: bfloat16 [24576, 4096], P('dp', 'expert'), may hold values from -6 to 6
- kv_cotangent: bfloat16 [24576, 1024], P('dp')
- expert_hidden: bfloat16 [3072, 12288], P('expert', 'dp')
- expert_cotangent: bfloat16 [3072, 131072], P('expert', 'dp'), may hold values from -6 to 6
- token_counts: int32 [64, 8], P('dp', 'expert'), may hold values from 1 to 384, 1728 in all within a row
- att_param: float32 [1024, 4096], P('dp', 'expert'), may hold values from -4 to 4
- att_moment: float32 [1024, 4096], P('dp', 'expert'), may hold values from -6 to 6
- att_second: float32 [1024, 4096], P('dp', 'expert'), may hold values from 0.2 to 4
- exp_param: float32 [12288, 2048], P(('dp', 'expert')), may hold values from -4 to 4
- exp_moment: float32 [12288, 2048], P(('dp', 'expert')), may hold values from -6 to 6
- exp_second: float32 [12288, 2048], P(('dp', 'expert')), may hold values from 0.2 to 4
Outputs:
- new_att_param: float32 [1024, 4096], P('dp', 'expert')
- new_att_moment: float32 [1024, 4096], P('dp', 'expert')
- new_att_second: float32 [1024, 4096], P('dp', 'expert')
- new_exp_param: float32 [12288, 2048], P(('dp', 'expert'))
- new_exp_moment: float32 [12288, 2048], P(('dp', 'expert'))
- new_exp_second: float32 [12288, 2048], P(('dp', 'expert'))
Inputs may be any that keep to these rules, and one draw needn't show every extreme that they name: Each row of token_counts sums to 1728, and its largest entry is 384.
All inputs are finite; a program needn't handle non-finite values. No bound on the sum of `token_counts` on one device may be relied on, other than what follows from the above.
Results may differ from a plain program's by a relative error of at most 0.0003.
Values sent between devices are 32-bit elements; how exact they have to be, the bound alone decides.
A program may use at most 64 MiB of HBM per device.

v0:
```python
import jax
import jax.numpy as jnp
from jax import lax
from jax.sharding import PartitionSpec as P

D = 4096
KV2 = 1024
FF = 1536
DW = 2048
GROUP = 8


beta_one = 0.9
beta_two = 0.95
learn_rate = 0.01
decay_rate = 0.1
epsilon = 1e-08
step_number = 5


def adam_update(param, moment, second, grad, clip):
    scaled = clip * grad
    new_moment = beta_one * moment + (1.0 - beta_one) * scaled
    new_second = beta_two * second + (1.0 - beta_two) * scaled * scaled
    fix_one = 1.0 - beta_one**step_number
    fix_two = 1.0 - beta_two**step_number
    update = new_moment / fix_one / (jnp.sqrt(new_second / fix_two) + epsilon)
    new_param = param - learn_rate * (update + decay_rate * param)
    return (new_param, new_moment, new_second)


def on_device(
    att_input,
    kv_cotangent,
    expert_hidden,
    expert_cotangent,
    token_counts,
    att_param,
    att_moment,
    att_second,
    exp_param,
    exp_moment,
    exp_second,
):
    token_rows = expert_hidden.shape[0]
    live_rows = jnp.arange(token_rows, dtype=jnp.int32) < token_counts[0, 0]
    masked_hidden = jnp.where(live_rows[:, None], expert_hidden, jnp.zeros((), jnp.bfloat16))
    columns = kv_cotangent
    att_grad = lax.psum_scatter(
        lax.dot_general(
            columns, att_input, (((0,), (0,)), ((), ())), preferred_element_type=jnp.float32
        ),
        "dp",
        scatter_dimension=0,
        tiled=True,
    )
    own_rows = exp_param.shape[0]
    columns = masked_hidden
    summed = lax.psum(
        lax.dot_general(
            columns, expert_cotangent, (((0,), (0,)), ((), ())), preferred_element_type=jnp.float32
        ),
        "expert",
    )
    exp_grad = lax.dynamic_slice_in_dim(summed, lax.axis_index("expert") * own_rows, own_rows, 0)
    att_squares = jnp.sum(att_grad * att_grad)
    exp_squares = jnp.sum(exp_grad * exp_grad)
    att_total = lax.psum(att_squares, ("dp", "expert"))
    exp_total = lax.psum(exp_squares, ("dp", "expert"))
    square_sum = att_total + exp_total
    entries = float(KV2 * D + lax.axis_size("dp") // GROUP * FF * DW)
    clip = jnp.minimum(1.0, jnp.sqrt(entries) / (jnp.sqrt(square_sum) + 1e-06))
    new_att = adam_update(att_param, att_moment, att_second, att_grad, clip)
    new_exp = adam_update(exp_param, exp_moment, exp_second, exp_grad, clip)
    return (new_att[0], new_att[1], new_att[2], new_exp[0], new_exp[1], new_exp[2])


def solution(mesh):
    in_specs = (
        P("dp", "expert"),
        P("dp", None),
        P("expert", "dp"),
        P("expert", "dp"),
        P("dp", "expert"),
        P("dp", "expert"),
        P("dp", "expert"),
        P("dp", "expert"),
        P(("dp", "expert"), None),
        P(("dp", "expert"), None),
        P(("dp", "expert"), None),
    )
    out_specs = (
        P("dp", "expert"),
        P("dp", "expert"),
        P("dp", "expert"),
        P(("dp", "expert"), None),
        P(("dp", "expert"), None),
        P(("dp", "expert"), None),
    )
    return jax.shard_map(
        on_device, mesh=mesh, in_specs=in_specs, out_specs=out_specs, check_vma=False
    )
```

profile of v0, /device:TPU:1, one launch (start us, length us, event | category | flops | bytes accessed | tf_op | source)
XLA Modules:
  0.0 282.3 jit_solution(4237121850248727597)
XLA Ops:
  8.0 0.0 copy-start
  8.0 0.0 all-reduce.2.cloned.1.call-start
  8.8 0.6 copy-done
  9.4 2.6 fusion.1
  12.1 0.0 all-reduce.2.cloned.1.call-update
  12.1 0.0 reduce-scatter.2.cloned.1.call-start
  12.1 1.1 copy-done.1
  13.2 0.1 copy-done.2
  13.3 2.1 fusion.9
  15.4 0.0 copy-start.4
  15.4 0.0 copy-start.5
  15.4 0.0 reduce-scatter.2.cloned.1.call-update
  15.4 83.3 %all-reduce.2.cloned.1.call-done = f32[192,2048]{1,0:T(8,128)} async-done(((f32[192,2048]{1,0:T(8,128)}), f32[192,2048]{1,0:T(8,128)}) %all-reduce.2.cloned.1.call-update) | async-done | bytes 1572880 | tf_op jit(solution)/shard_map/psum | solution.py:59
  98.8 1.6 multiply_reduce_fusion
  100.3 65.6 %reduce-scatter.2.cloned.1.call-done = f32[16,512]{1,0:T(8,128)} async-done(((f32[1024,512]{1,0:T(8,128)}), f32[16,512]{1,0:T(8,128)}) %reduce-scatter.2.cloned.1.call-update) | async-done | bytes 32784 | tf_op jit(solution)/shard_map/reduce_scatter | solution.py:49
  166.0 1.4 multiply_reduce_fusion.1
  168.7 102.2 %psum.24 = f32[]{:T(128)} all-reduce(f32[]{:T(128)S(6)} %add.48), channel_id=1, replica_groups=mesh['dp'=64,'expert'=8] {'dp','expert'}, use_global_device_ids=true, to_apply=%region_2.3 | all-reduce | flops 1 | bytes 8 | tf_op jit(solution)/shard_map/psum | solution.py:68
  271.6 0.0 copy-done.6
  271.6 0.0 copy-done.7
  271.6 0.0 copy-done.8
  271.6 1.4 multiply_subtract_fusion.1
  273.0 0.0 copy-done.3
  273.0 0.0 copy-done.4
  273.0 1.8 multiply_subtract_fusion
  (8 shorter events, 0.0 us)
Async XLA Ops:
  8.0 1.4 copy-start
  8.0 90.8 %all-reduce.2.cloned.1.call-start = ((), (), s32[]{:S(2)}) async-start(), calls=%async_computation.2 | async-start | bytes 3145728 | tf_op jit(solution)/shard_map/psum | solution.py:59
  12.1 1.1 copy-start.1
  12.1 1.2 copy-start.2
  12.1 153.9 %reduce-scatter.2.cloned.1.call-start = ((), (), s32[]{:S(2)}) async-start(), calls=%async_computation.1 | async-start | bytes 2129920 | tf_op jit(solution)/shard_map/reduce_scatter | solution.py:49
  15.4 256.2 %copy-start.6 = (f32[16,512]{1,0:T(8,128)S(1)}, f32[16,512]{1,0:T(8,128)}, u32[]{:S(2)}) copy-start(f32[16,512]{1,0:T(8,128)} %param.16) | copy-start | bytes 98308
  15.4 256.2 %copy-start.7 = (f32[16,512]{1,0:T(8,128)S(1)}, f32[16,512]{1,0:T(8,128)}, u32[]{:S(2)}) copy-start(f32[16,512]{1,0:T(8,128)} %param.17) | copy-start | bytes 98308
  15.4 256.2 %copy-start.8 = (f32[16,512]{1,0:T(8,128)S(1)}, f32[16,512]{1,0:T(8,128)}, u32[]{:S(2)}) copy-start(f32[16,512]{1,0:T(8,128)} %param.18) | copy-start | bytes 98308
  15.4 257.6 %copy-start.3 = (f32[24,2048]{1,0:T(8,128)S(1)}, f32[24,2048]{1,0:T(8,128)}, u32[]{:S(2)}) copy-start(f32[24,2048]{1,0:T(8,128)} %param.19) | copy-start | bytes 589828
  15.4 257.6 %copy-start.4 = (f32[24,2048]{1,0:T(8,128)S(1)}, f32[24,2048]{1,0:T(8,128)}, u32[]{:S(2)}) copy-start(f32[24,2048]{1,0:T(8,128)} %param.20) | copy-start | bytes 589828
  15.4 257.6 %copy-start.5 = (f32[24,2048]{1,0:T(8,128)S(1)}, f32[24,2048]{1,0:T(8,128)}, u32[]{:S(2)}) copy-start(f32[24,2048]{1,0:T(8,128)} %param.21) | copy-start | bytes 589828
Sparse Core Ops, SparseCore 0:
  12.2 86.4 all-reduce.1
Sparse Core Ops, SparseCore 1:
  17.2 148.7 reduce-scatter.1
where the time goes:
time: 283 us; the launch traced here: 282 us
  waiting for transfers between devices  149 us (53%)
  blocking collectives  102 us (36%)
  between operations  18.3 us (6%)
  other arithmetic  6.21 us (2%)
  matrix products  4.72 us (2%)
    psum x1, blocking collectives, on_device(): att_total = lax.psum(att_squares, ('dp', 'expert'))  102 us
    psum x1, waiting for transfers between devices, on_device(): lax.psum(lax.dot_general(columns, expert_cotangent, (((0,), (0,)), ((), (...  83.3 us
    reduce_scatter x1, waiting for transfers between devices, on_device(): lax.psum_scatter(lax.dot_general(columns, att_input, (((0,), (0,)), ((),...  65.6 us
  transfers between devices with their start and end apart: 2, of which 2 were waited for; matrix products, arithmetic and copies ran while one was open for 1% of the time, Pallas kernels for 0%

commit v1 on v0

v1 whole, which is shorter than its diff:
```python
import functools

import jax
import jax.numpy as jnp
from jax import lax
from jax.experimental import pallas as pl
from jax.experimental.pallas import tpu as pltpu
from jax.sharding import PartitionSpec as P

D = 4096
KV2 = 1024
FF = 1536
DW = 2048
GROUP = 8

beta_one = 0.9
beta_two = 0.95
learn_rate = 0.01
decay_rate = 0.1
epsilon = 1e-08
step_number = 5

NX, NY, NZ, NC = 4, 8, 8, 2
TOK = 384
HID = 192
OWN = HID // NZ
PIECES = 4
WIDE = DW // PIECES
COLS = 512
HALF = COLS // 2
ROWS = 16
GROUPS = 4
Y_ORDER = (4, 3, 5, 2, 6, 1, 7, 0)
NORM_STEPS = ((NZ, 1, 1, 1), (1, NY, 1, 1), (1, 1, NX, NC))
NORM_PEERS = tuple(a * b * c * d for a, b, c, d in NORM_STEPS)
MESH = pl.DeviceIdType.MESH


def grads_kernel(
    hidden_hbm, cot_hbm, kv_hbm, x_hbm, count_ref,
    exp_ref, att_ref, norm_ref,
    hidden, cot, kv, xin, masked, part, ring, grad, core_in, keep, send_a, recv_a, keep_b, send_b, recv_b, y_out, y_in,
    norm_a, norm_b, norm_c,
    load_sem, ring_send, ring_recv, core_send, core_recv, a_send, a_recv, b_send, b_recv, y_send, y_recv, norm_send, norm_recv,
):
    dp = lax.axis_index("dp")
    z = lax.axis_index("expert")
    c = lax.rem(dp, NC)
    x = lax.rem(dp // NC, NX)
    y = dp // (NC * NX)

    def at(zz, yy, xx, cc):
        return ((yy * NX + xx) * NC + cc, zz)

    x_rel = (x, x + 1 - 2 * lax.rem(x, 2), lax.rem(x + 2, NX), NX - 1 - x)

    barrier = pltpu.get_barrier_semaphore()
    greeted = [at(lax.rem(z + 1, NZ), y, x, c), at(lax.rem(z + NZ - 1, NZ), y, x, c), at(z, y, x, 1 - c)]
    greeted += [at(z, y, x_rel[1], c), at(z, y, x_rel[3], c)]
    greeted += [at(z, lax.rem(y + d, NY), x, c) for d in range(1, NY)]
    for device in greeted:
        pl.semaphore_signal(barrier, inc=1, device_id=device, device_id_type=MESH)

    loads = [pltpu.make_async_copy(hidden_hbm, hidden, load_sem.at[0])]
    for k in range(PIECES):
        loads.append(pltpu.make_async_copy(cot_hbm.at[:, pl.ds(k * WIDE, WIDE)], cot.at[k], load_sem.at[1 + k]))
    loads.append(pltpu.make_async_copy(x_hbm, xin, load_sem.at[1 + PIECES]))
    loads.append(pltpu.make_async_copy(kv_hbm, kv, load_sem.at[2 + PIECES]))
    for load in loads:
        load.start()

    sends = []

    def remote(src, dst, send_sem, recv_sem, device):
        copy = pltpu.make_async_remote_copy(
            src_ref=src, dst_ref=dst, send_sem=send_sem, recv_sem=recv_sem, device_id=device, device_id_type=MESH
        )
        copy.start()
        sends.append(copy)
        return copy

    def shard(k, t):
        return lax.rem(z + NZ - 1 - t, NZ) if k % 2 == 0 else lax.rem(z + 1 + t, NZ)

    def ring_to(k):
        return at(lax.rem(z + 1, NZ) if k % 2 == 0 else lax.rem(z + NZ - 1, NZ), y, x, c)

    arrivals = {}

    def ring_send_step(k, t):
        src = part.at[k, shard(k, 0)] if t == 0 else ring.at[k, t - 1]
        arrivals[k, t] = remote(src, ring.at[k, t], ring_send.at[k, t], ring_recv.at[k, t], ring_to(k))

    def ring_step(k, t):
        arrivals[k, t].wait_recv()
        ring[k, t] = ring[k, t] + part[k, shard(k, t + 1)]
        ring_send_step(k, t + 1)

    loads[0].wait()
    live = lax.broadcasted_iota(jnp.int32, (TOK, HID), 0) < count_ref[0, 0]
    masked[...] = jnp.where(live, hidden[...].astype(jnp.float32), 0.0).astype(jnp.bfloat16)

    def exp_piece(k):
        loads[1 + k].wait()
        block = lax.dot_general(
            masked[...], cot[k], (((0,), (0,)), ((), ())), preferred_element_type=jnp.float32
        )
        part[k] = block.reshape(NZ, OWN, WIDE)
        if k == 0:
            pl.semaphore_wait(barrier, len(greeted))
        ring_send_step(k, 0)

    core_copy, a_copy, b_copy = {}, {}, {}

    def att_group(g):
        if g == 0:
            loads[1 + PIECES].wait()
            loads[2 + PIECES].wait()
        for i in (2 * g, 2 * g + 1):
            target = lax.rem(y + Y_ORDER[i], NY)
            columns = kv[:, pl.ds(pl.multiple_of(target * (KV2 // NY), KV2 // NY), KV2 // NY)]
            block = lax.dot_general(columns, xin[...], (((0,), (0,)), ((), ())), preferred_element_type=jnp.float32)
            grad[i] = block.reshape(NX, NC, ROWS, COLS)
        core_copy[g] = remote(
            grad.at[pl.ds(2 * g, 2), :, 1 - c], core_in.at[g], core_send.at[g], core_recv.at[g], at(z, y, x, 1 - c)
        )

    slots = ((0, 3, 1, 2), (0, 1, 3, 2))
    first_to = (x_rel[1], x_rel[3])
    second_to = (x_rel[3], x_rel[1])

    def att_first(g):
        core_copy[g].wait_recv()
        for h in range(2):
            cols = pl.ds(h * HALF, HALF)
            for j in (2, 3):
                at_x = x_rel[slots[h][j]]
                for i in range(2):
                    send_a[g, h, j - 2, i] = grad[2 * g + i, at_x, c, :, cols] + core_in[g, i, at_x, :, cols]
            a_copy[g, h] = remote(
                send_a.at[g, h], recv_a.at[g, h], a_send.at[g, h], a_recv.at[g, h], at(z, y, first_to[h], c)
            )
        for h in range(2):
            cols = pl.ds(h * HALF, HALF)
            for j in (0, 1):
                at_x = x_rel[slots[h][j]]
                for i in range(2):
                    keep[g, h, j, i] = grad[2 * g + i, at_x, c, :, cols] + core_in[g, i, at_x, :, cols]

    def att_second(g):
        for h in range(2):
            a_copy[g, h].wait_recv()
            send_b[g, h] = keep[g, h, 1] + recv_a[g, h, 1]
            b_copy[g, h] = remote(
                send_b.at[g, h], recv_b.at[g, h], b_send.at[g, h], b_recv.at[g, h], at(z, y, second_to[h], c)
            )
            keep_b[g, h] = keep[g, h, 0] + recv_a[g, h, 0]

    y_copy = {}

    def att_third(g):
        for h in range(2):
            b_copy[g, h].wait_recv()
            for i in range(2):
                y_out[2 * g + i, :, pl.ds(h * HALF, HALF)] = keep_b[g, h, i] + recv_b[g, h, i]
        for i in (2 * g, 2 * g + 1):
            d = Y_ORDER[i]
            if d:
                y_copy[d] = remote(
                    y_out.at[i], y_in.at[d - 1], y_send.at[d - 1], y_recv.at[d - 1], at(z, lax.rem(y + d, NY), x, c)
                )

    def att_last():
        total = y_out[Y_ORDER.index(0)]
        for d in Y_ORDER:
            if d:
                y_copy[d].wait_recv()
                total = total + y_in[d - 1]
        att_ref[...] = total
        return jnp.sum(total * total, axis=0, keepdims=True)

    def steps(t, *pieces):
        for k in pieces or range(PIECES):
            ring_step(k, t)

    for k in range(PIECES):
        exp_piece(k)
    att_group(0)
    att_group(1)
    steps(0, 0, 1)
    att_group(2)
    steps(0, 2, 3)
    att_group(3)
    att_first(0)
    steps(1, 0, 1)
    att_first(1)
    steps(1, 2, 3)
    att_first(2)
    steps(2, 0, 1)
    att_first(3)
    att_second(0)
    steps(2, 2, 3)
    att_second(1)
    steps(3, 0, 1)
    att_second(2)
    att_third(0)
    steps(3, 2, 3)
    att_third(1)
    steps(4, 0, 1)
    att_second(3)
    att_third(2)
    steps(4, 2, 3)
    steps(5, 0, 1)
    att_third(3)
    steps(5, 2, 3)

    att_squares = att_last()
    squares = att_squares[:, 0:128]
    for j in range(1, COLS // 128):
        squares = squares + att_squares[:, j * 128 : (j + 1) * 128]
    for k in range(PIECES):
        arrivals[k, NZ - 2].wait_recv()
        total = ring[k, NZ - 2] + part[k, z]
        exp_ref[:, pl.ds(k * WIDE, WIDE)] = total
        sums = jnp.sum(total * total, axis=0, keepdims=True)
        for j in range(WIDE // 128):
            squares = squares + sums[:, j * 128 : (j + 1) * 128]

    value = squares
    for n, (extent, peers, buffer) in enumerate(zip(NORM_STEPS, NORM_PEERS, (norm_a, norm_b, norm_c))):
        buffer[0] = value
        slot = 0
        for dz in range(extent[0]):
            for dy in range(extent[1]):
                for dx in range(extent[2]):
                    for dc in range(extent[3]):
                        if slot:
                            device = at(
                                lax.rem(z + dz, NZ), lax.rem(y + dy, NY), lax.rem(x + dx, NX), lax.rem(c + dc, NC)
                            )
                            pltpu.make_async_remote_copy(
                                src_ref=buffer.at[0],
                                dst_ref=buffer.at[slot],
                                send_sem=norm_send.at[n],
                                recv_sem=norm_recv.at[n],
                                device_id=device,
                                device_id_type=MESH,
                            ).start()
                        slot += 1
        others = buffer.at[pl.ds(1, peers - 1)]
        pltpu.make_async_copy(others, others, norm_recv.at[n]).wait()
        value = jnp.sum(buffer[...], axis=0)
    norm_ref[...] = value

    for copy in sends:
        copy.wait_send()
    for n, (peers, buffer) in enumerate(zip(NORM_PEERS, (norm_a, norm_b, norm_c))):
        others = buffer.at[pl.ds(1, peers - 1)]
        pltpu.make_async_copy(others, others, norm_send.at[n]).wait()


def grads(hidden, cot, kv, xin, counts):
    f32, bf16 = jnp.float32, jnp.bfloat16
    dma = pltpu.SemaphoreType.DMA
    hbm = pl.BlockSpec(memory_space=pl.ANY)
    vmem = pl.BlockSpec(memory_space=pltpu.VMEM)
    return pl.pallas_call(
        grads_kernel,
        out_shape=(
            jax.ShapeDtypeStruct((OWN, DW), f32),
            jax.ShapeDtypeStruct((ROWS, COLS), f32),
            jax.ShapeDtypeStruct((1, 128), f32),
        ),
        in_specs=[hbm, hbm, hbm, hbm, pl.BlockSpec(memory_space=pltpu.SMEM)],
        out_specs=(vmem, vmem, vmem),
        scratch_shapes=[
            pltpu.VMEM((TOK, HID), bf16),
            pltpu.VMEM((PIECES, TOK, WIDE), bf16),
            pltpu.VMEM((TOK, KV2), bf16),
            pltpu.VMEM((TOK, COLS), bf16),
            pltpu.VMEM((TOK, HID), bf16),
            pltpu.VMEM((PIECES, NZ, OWN, WIDE), f32),
            pltpu.VMEM((PIECES, NZ - 1, OWN, WIDE), f32),
            pltpu.VMEM((NY, NX, NC, ROWS, COLS), f32),
            pltpu.VMEM((GROUPS, 2, NX, ROWS, COLS), f32),
            pltpu.VMEM((GROUPS, 2, 2, 2, ROWS, HALF), f32),
            pltpu.VMEM((GROUPS, 2, 2, 2, ROWS, HALF), f32),
            pltpu.VMEM((GROUPS, 2, 2, 2, ROWS, HALF), f32),
            pltpu.VMEM((GROUPS, 2, 2, ROWS, HALF), f32),
            pltpu.VMEM((GROUPS, 2, 2, ROWS, HALF), f32),
            pltpu.VMEM((GROUPS, 2, 2, ROWS, HALF), f32),
            pltpu.VMEM((NY, ROWS, COLS), f32),
            pltpu.VMEM((NY - 1, ROWS, COLS), f32),
            pltpu.VMEM((NORM_PEERS[0], 1, 128), f32),
            pltpu.VMEM((NORM_PEERS[1], 1, 128), f32),
            pltpu.VMEM((NORM_PEERS[2], 1, 128), f32),
            dma((3 + PIECES,)),
            dma((PIECES, NZ - 1)),
            dma((PIECES, NZ - 1)),
            dma((GROUPS,)),
            dma((GROUPS,)),
            dma((GROUPS, 2)),
            dma((GROUPS, 2)),
            dma((GROUPS, 2)),
            dma((GROUPS, 2)),
            dma((NY - 1,)),
            dma((NY - 1,)),
            dma((3,)),
            dma((3,)),
        ],
        compiler_params=pltpu.CompilerParams(
            collective_id=0, has_side_effects=True, vmem_limit_bytes=24 * 1024 * 1024
        ),
        name="grads",
    )(hidden, cot, kv, xin, counts)


def adam_update(param, moment, second, grad, clip):
    scaled = clip * grad
    new_moment = beta_one * moment + (1.0 - beta_one) * scaled
    new_second = beta_two * second + (1.0 - beta_two) * scaled * scaled
    fix_one = 1.0 - beta_one**step_number
    fix_two = 1.0 - beta_two**step_number
    update = new_moment / fix_one / (jnp.sqrt(new_second / fix_two) + epsilon)
    new_param = param - learn_rate * (update + decay_rate * param)
    return (new_param, new_moment, new_second)


def update_kernel(norm_ref, *refs):
    entries = float(KV2 * D + NY * NX * NC // GROUP * FF * DW)
    square_sum = jnp.sum(norm_ref[...], axis=1, keepdims=True)
    clip = jnp.minimum(1.0, jnp.sqrt(jnp.full_like(square_sum, entries)) / (jnp.sqrt(square_sum) + 1e-06))
    for n in range(2):
        param, moment, second, grad = refs[4 * n : 4 * n + 4]
        new = adam_update(param[...], moment[...], second[...], grad[...], clip)
        for ref, value in zip(refs[8 + 3 * n : 11 + 3 * n], new):
            ref[...] = value


def update(norm, att, exp):
    shapes = [jax.ShapeDtypeStruct(a.shape, a.dtype) for a in (*att[:3], *exp[:3])]
    vmem = pl.BlockSpec(memory_space=pltpu.VMEM)
    return pl.pallas_call(
        update_kernel,
        out_shape=tuple(shapes),
        in_specs=[vmem] * 9,
        out_specs=(vmem,) * 6,
        name="update",
    )(norm, *att, *exp)


def on_device(
    att_input,
    kv_cotangent,
    expert_hidden,
    expert_cotangent,
    token_counts,
    att_param,
    att_moment,
    att_second,
    exp_param,
    exp_moment,
    exp_second,
):
    exp_grad, att_grad, norm = grads(expert_hidden, expert_cotangent, kv_cotangent, att_input, token_counts)
    return update(
        norm,
        (att_param, att_moment, att_second, att_grad),
        (exp_param, exp_moment, exp_second, exp_grad),
    )


def solution(mesh):
    in_specs = (
        P("dp", "expert"),
        P("dp", None),
        P("expert", "dp"),
        P("expert", "dp"),
        P("dp", "expert"),
        P("dp", "expert"),
        P("dp", "expert"),
        P("dp", "expert"),
        P(("dp", "expert"), None),
        P(("dp", "expert"), None),
        P(("dp", "expert"), None),
    )
    out_specs = (
        P("dp", "expert"),
        P("dp", "expert"),
        P("dp", "expert"),
        P(("dp", "expert"), None),
        P(("dp", "expert"), None),
        P(("dp", "expert"), None),
    )
    return jax.shard_map(
        on_device, mesh=mesh, in_specs=in_specs, out_specs=out_specs, check_vma=False
    )
```

time: 283 us -> 63.7 us (0.23)
  waiting for transfers between devices: 149 us -> 0 us
  blocking collectives: 102 us -> 0 us
  Pallas kernels: 0 us -> 55.8 us
  between operations: 18.3 us -> 1.31 us
  other arithmetic: 6.21 us -> 0 us
  matrix products: 4.72 us -> 0 us
  local copies, waits for them, and re-layouts: 1.79 us -> 6.36 us
    psum x1 -> x0, blocking collectives: 102 us -> none  [on_device(): att_total = lax.psum(att_squares, ('dp', 'expert'))]
    psum x1 -> x0, waiting for transfers between devices: 83.3 us -> none  [on_device(): lax.psum(lax.dot_general(columns, expert_cotangent, (((0,), (0,)), ((), (...]
    reduce_scatter x1 -> x0, waiting for transfers between devices: 65.6 us -> none  [on_device(): lax.psum_scatter(lax.dot_general(columns, att_input, (((0,), (0,)), ((),...]
    pallas_call x0 -> x2, Pallas kernels: none -> 55.8 us  [the longest x1 53.4 us: grads(): pl.pallas_call(grads_kernel, out_shape=(jax.ShapeDtypeStruct((OWN, DW), f...]
    dot_general x2 -> x0, matrix products: 4.72 us -> none  [the longest x1 2.64 us: on_device(): lax.dot_general(columns, expert_cotangent, (((0,), (0,)), ((), ())), pref...]
    unnamed x18 -> x13, local copies, waits for them, and re-layouts: 1.79 us -> 6.36 us
    sub x2 -> x0, other arithmetic: 3.25 us -> none  [adam_update(): new_param = param - learn_rate * (update + decay_rate * param)]
    reduce_sum x2 -> x0, other arithmetic: 2.95 us -> none  [the longest x1 1.58 us: on_device(): exp_squares = jnp.sum(exp_grad * exp_grad)]
  transfers between devices with their start and end apart: 2 -> 0, of which waited for: 2 -> 0; matrix products, arithmetic and copies ran while one was open for 1% -> 0% of each run, Pallas kernels for 0% -> 0%
where the time goes in v1:
time: 63.7 us; the launch traced here: 63.4 us
  Pallas kernels  55.8 us (88%)
  local copies, waits for them, and re-layouts  6.36 us (10%)
  between operations  1.31 us (2%)
    pallas_call x1, Pallas kernels, grads(): pl.pallas_call(grads_kernel, out_shape=(jax.ShapeDtypeStruct((OWN, DW), f...  53.4 us
    unnamed x13, local copies, waits for them, and re-layouts  6.36 us
    pallas_call x1, Pallas kernels, update(): pl.pallas_call(update_kernel, out_shape=tuple(shapes), in_specs=[vmem] *...  2.36 us

profile of v1, /device:TPU:1, one launch (start us, length us, event | category | flops | bytes accessed | tf_op | source)
XLA Modules:
  0.0 63.4 jit_solution(4808871848606424752)
XLA Ops:
  1.3 1.0 %copy.17.hidden_hbm = bf16[384,192]{1,0:T(8,128)(2,1)S(1)} copy(bf16[384,192]{0,1:T(8,128)(2,1)} %param.13) | data formatting | bytes 294912 | tf_op args[2]
  2.3 0.0 copy-start
  2.3 1.4 %copy-done = bf16[384,2048]{1,0:T(8,128)(2,1)S(1)} copy-done((bf16[384,2048]{1,0:T(8,128)(2,1)S(1)}, bf16[384,2048]{1,0:T(8,128)(2,1)}, u32[]{:S(2)}) %copy-start) | copy-done | bytes 1572888
  3.7 0.0 copy-start.1
  3.7 1.1 %copy-done.1 = bf16[384,1024]{1,0:T(8,128)(2,1)S(1)} copy-done((bf16[384,1024]{1,0:T(8,128)(2,1)S(1)}, bf16[384,1024]{1,0:T(8,128)(2,1)}, u32[]{:S(2)}) %copy-start.1) | copy-done | bytes 786456
  4.9 0.0 copy-start.2
  4.9 1.0 %copy-done.2 = bf16[384,512]{1,0:T(8,128)(2,1)S(1)} copy-done((bf16[384,512]{1,0:T(8,128)(2,1)S(1)}, bf16[384,512]{1,0:T(8,128)(2,1)}, u32[]{:S(2)}) %copy-start.2) | copy-done | bytes 393240
  5.9 53.4 %grads.1 = (f32[24,2048]{1,0:T(8,128)S(1)}, f32[16,512]{1,0:T(8,128)S(1)}, f32[1,128]{1,0:T(1,128)S(1)}) custom-call(bf16[384,192]{1,0:T(8,128)(2,1)S(1)} %copy.17.hidden_hbm, bf16[384,2048]{1,0:T(8,128)(2,1)S(1)} %copy-done, bf16[384,1024]{1,0:T(8,128)(2,1)S(1)} %copy-done.1, bf16[384,512]{1,0:T(8,128)(2,1)S(1)} %copy-done.2, s32[1,1]{1,0:T(1,128)S(6)} %copy.18.count_ref), custom_call_target="tpu_custom_call" | custom-call | tf_op jit(solution)/shard_map/grads/pallas_call | solution.py:267
  59.3 0.0 copy-start.3
  59.3 0.7 %copy-done.3 = f32[24,2048]{1,0:T(8,128)} copy-done((f32[24,2048]{1,0:T(8,128)}, f32[24,2048]{1,0:T(8,128)S(1)}, u32[]{:S(2)}) %copy-start.3) | copy-done | bytes 196632
  60.0 0.0 copy-start.4
  60.0 0.6 copy-done.4
  60.6 0.0 copy-start.5
  60.6 0.5 copy-done.5
  61.1 2.4 %update.1 = (f32[16,512]{1,0:T(8,128)}, f32[16,512]{1,0:T(8,128)}, f32[16,512]{1,0:T(8,128)}, f32[24,2048]{1,0:T(8,128)}, f32[24,2048]{1,0:T(8,128)}, /*index=5*/f32[24,2048]{1,0:T(8,128)}) custom-call(f32[1,128]{1,0:T(1,128)} %copy-done.5, f32[16,512]{1,0:T(8,128)} %refs_0_.1, f32[16,512]{1,0:T(8,128)} %refs_1_.1, f32[16,512]{1,0:T(8,128)} %refs_2_.1, ...), custom_call_target="tpu_custom_call" | custom-call | tf_op jit(solution)/shard_map/update/pallas_call | solution.py:343
Async XLA Ops:
  2.3 1.4 %copy-start = (bf16[384,2048]{1,0:T(8,128)(2,1)S(1)}, bf16[384,2048]{1,0:T(8,128)(2,1)}, u32[]{:S(2)}) copy-start(bf16[384,2048]{1,0:T(8,128)(2,1)} %cot_hbm.1) | copy-start | bytes 4718596
  3.7 1.1 %copy-start.1 = (bf16[384,1024]{1,0:T(8,128)(2,1)S(1)}, bf16[384,1024]{1,0:T(8,128)(2,1)}, u32[]{:S(2)}) copy-start(bf16[384,1024]{1,0:T(8,128)(2,1)} %kv_hbm.1) | copy-start | bytes 2359300
  4.9 1.0 %copy-start.2 = (bf16[384,512]{1,0:T(8,128)(2,1)S(1)}, bf16[384,512]{1,0:T(8,128)(2,1)}, u32[]{:S(2)}) copy-start(bf16[384,512]{1,0:T(8,128)(2,1)} %x_hbm.1) | copy-start | bytes 1179652
  59.3 0.7 %copy-start.3 = (f32[24,2048]{1,0:T(8,128)}, f32[24,2048]{1,0:T(8,128)S(1)}, u32[]{:S(2)}) copy-start(f32[24,2048]{1,0:T(8,128)S(1)} %get-tuple-element.11.refs_7_) | copy-start | bytes 589828
  60.0 0.6 copy-start.4
  60.6 0.5 copy-start.5

commit v2 on v1

v2 whole, which is shorter than its diff:
```python
import functools

import jax
import jax.numpy as jnp
from jax import lax
from jax.experimental import pallas as pl
from jax.experimental.pallas import tpu as pltpu
from jax.sharding import PartitionSpec as P

D = 4096
KV2 = 1024
FF = 1536
DW = 2048
GROUP = 8

beta_one = 0.9
beta_two = 0.95
learn_rate = 0.01
decay_rate = 0.1
epsilon = 1e-08
step_number = 5

NX, NY, NZ, NC = 4, 8, 8, 2
TOK = 384
HID = 192
OWN = HID // NZ
HALVES = 2
SPLIT = 2
PIECES = HALVES * SPLIT
WIDE = DW // PIECES
DEPTH = NZ // 2
COLS = 512
HALF = COLS // 2
ROWS = 16
GROUPS = 4
Y_ORDER = (4, 3, 5, 2, 6, 1, 7, 0)
MESH = pl.DeviceIdType.MESH
BETWEEN = {
    3: (("second", 0),),
    5: (("second", 1),),
    6: (("second", 2),),
    8: (("second", 3), ("third", 0)),
    9: (("third", 1),),
    10: (("third", 2),),
    11: (("third", 3),),
    12: (("last", 0),),
}


def adam_update(param, moment, second, grad, clip):
    scaled = clip * grad
    new_moment = beta_one * moment + (1.0 - beta_one) * scaled
    new_second = beta_two * second + (1.0 - beta_two) * scaled * scaled
    fix_one = 1.0 - beta_one**step_number
    fix_two = 1.0 - beta_two**step_number
    update = new_moment / fix_one / (jnp.sqrt(new_second / fix_two) + epsilon)
    new_param = param - learn_rate * (update + decay_rate * param)
    return (new_param, new_moment, new_second)


def grads_kernel(
    hidden_hbm, cot_hbm, kv_hbm, x_hbm, count_hbm,
    exp_hbm, att_hbm, norm_ref,
    exp_ref, att_ref, count_ref, hidden, cot, kv, xin, masked, part, ring, grad, core_in, keep, send_a, recv_a, keep_b, send_b, recv_b, y_out, y_in,
    norm_c, norm_z, norm_p,
    load_sem, ring_send, ring_recv, core_send, core_recv, a_send, a_recv, b_send, b_recv, y_send, y_recv, norm_send, norm_recv, out_sem,
):
    dp = lax.axis_index("dp")
    z = lax.axis_index("expert")
    c = lax.rem(dp, NC)
    x = lax.rem(dp // NC, NX)
    y = dp // (NC * NX)

    def at(zz, yy, xx, cc):
        return ((yy * NX + xx) * NC + cc, zz)

    x_rel = (x, x + 1 - 2 * lax.rem(x, 2), lax.rem(x + 2, NX), NX - 1 - x)

    barrier = pltpu.get_barrier_semaphore()
    greeted = [at(lax.rem(z + 1, NZ), y, x, c), at(lax.rem(z + NZ - 1, NZ), y, x, c), at(z, y, x, 1 - c)]
    greeted += [at(z, y, x_rel[1], c), at(z, y, x_rel[3], c)]
    greeted += [at(z, lax.rem(y + d, NY), x, c) for d in range(1, NY)]
    for device in greeted:
        pl.semaphore_signal(barrier, inc=1, device_id=device, device_id_type=MESH)

    loads = [pltpu.make_async_copy(hidden_hbm, hidden, load_sem.at[0])]
    for k in range(PIECES):
        loads.append(pltpu.make_async_copy(cot_hbm.at[:, pl.ds(k * WIDE, WIDE)], cot.at[k], load_sem.at[1 + k]))
    loads.append(pltpu.make_async_copy(x_hbm, xin, load_sem.at[1 + PIECES]))
    loads.append(pltpu.make_async_copy(kv_hbm, kv, load_sem.at[2 + PIECES]))
    count_load = pltpu.make_async_copy(count_hbm, count_ref, load_sem.at[3 + PIECES])
    count_load.start()
    for load in loads:
        load.start()

    def squares_of(value):
        rows, width = value.shape
        value = value * value
        total = value[0:8, 0:128]
        for i in range(0, rows, 8):
            for j in range(0, width, 128):
                if i or j:
                    total = total + value[i : i + 8, j : j + 128]
        return total

    sends = []

    def remote(src, dst, send_sem, recv_sem, device):
        copy = pltpu.make_async_remote_copy(
            src_ref=src, dst_ref=dst, send_sem=send_sem, recv_sem=recv_sem, device_id=device, device_id_type=MESH
        )
        copy.start()
        sends.append(copy)
        return copy

    towards = (at(lax.rem(z + NZ - 1, NZ), y, x, c), at(lax.rem(z + 1, NZ), y, x, c))

    def shard(way, hops):
        return lax.rem(z + NZ - hops, NZ) if way == 0 else lax.rem(z + hops, NZ)

    arrivals = {}

    def ring_send_step(way, k, hops, src):
        arrivals[way, k, hops] = remote(
            src, ring.at[way, k, hops - 1], ring_send.at[way, k, hops - 1], ring_recv.at[way, k, hops - 1], towards[way]
        )

    def ring_start(way, k):
        hops = DEPTH if k // SPLIT == way else DEPTH - 1
        ring_send_step(way, k, hops, part.at[k, shard(way, hops)])

    squares, outs = [], []

    def ring_step(way, k, hops):
        arrivals[way, k, hops].wait_recv()
        left = hops - 1
        if left:
            ring[way, k, left] = ring[way, k, left] + part[k, shard(way, left)]
            ring_send_step(way, k, left, ring.at[way, k, left])
            return
        cols = pl.ds(k % PIECES * WIDE, WIDE)
        if k // SPLIT != way:
            exp_ref[:, cols] = part[k, z] + ring[way, k, 0]
        else:
            total = exp_ref[:, cols] + ring[way, k, 0]
            exp_ref[:, cols] = total
            outs.append(pltpu.make_async_copy(exp_ref.at[:, cols], exp_hbm.at[:, cols], out_sem.at[1 + k]))
            outs[-1].start()
            squares.append(squares_of(total))

    count_load.wait()
    loads[0].wait()
    live = lax.broadcasted_iota(jnp.int32, (HID, TOK), 1) < count_ref[0, 0]
    masked[...] = jnp.where(live, hidden[...].astype(jnp.float32), 0.0).astype(jnp.bfloat16)

    def exp_piece(k):
        loads[1 + k].wait()
        block = lax.dot_general(
            masked[...], cot[k], (((1,), (0,)), ((), ())), preferred_element_type=jnp.float32
        )
        part[k] = block.reshape(NZ, OWN, WIDE)

    core_copy, a_copy, b_copy = {}, {}, {}

    def att_group(g):
        if g == 0:
            loads[1 + PIECES].wait()
            loads[2 + PIECES].wait()
        for i in (2 * g, 2 * g + 1):
            target = lax.rem(y + Y_ORDER[i], NY)
            columns = kv[:, pl.ds(pl.multiple_of(target * (KV2 // NY), KV2 // NY), KV2 // NY)]
            block = lax.dot_general(columns, xin[...], (((0,), (0,)), ((), ())), preferred_element_type=jnp.float32)
            grad[i] = block.reshape(NX, NC, ROWS, COLS)
        core_copy[g] = remote(
            grad.at[pl.ds(2 * g, 2), :, 1 - c], core_in.at[g], core_send.at[g], core_recv.at[g], at(z, y, x, 1 - c)
        )

    slots = ((0, 3, 1, 2), (0, 1, 3, 2))
    first_to = (x_rel[1], x_rel[3])
    second_to = (x_rel[3], x_rel[1])

    def att_first(g):
        core_copy[g].wait_recv()
        for h in range(2):
            cols = pl.ds(h * HALF, HALF)
            for j in (2, 3):
                at_x = x_rel[slots[h][j]]
                for i in range(2):
                    send_a[g, h, j - 2, i] = grad[2 * g + i, at_x, c, :, cols] + core_in[g, i, at_x, :, cols]
            a_copy[g, h] = remote(
                send_a.at[g, h], recv_a.at[g, h], a_send.at[g, h], a_recv.at[g, h], at(z, y, first_to[h], c)
            )
        for h in range(2):
            cols = pl.ds(h * HALF, HALF)
            for j in (0, 1):
                at_x = x_rel[slots[h][j]]
                for i in range(2):
                    keep[g, h, j, i] = grad[2 * g + i, at_x, c, :, cols] + core_in[g, i, at_x, :, cols]

    def att_second(g):
        for h in range(2):
            a_copy[g, h].wait_recv()
            send_b[g, h] = keep[g, h, 1] + recv_a[g, h, 1]
            b_copy[g, h] = remote(
                send_b.at[g, h], recv_b.at[g, h], b_send.at[g, h], b_recv.at[g, h], at(z, y, second_to[h], c)
            )
            keep_b[g, h] = keep[g, h, 0] + recv_a[g, h, 0]

    y_copy = {}

    def att_third(g):
        for h in range(2):
            b_copy[g, h].wait_recv()
            for i in range(2):
                y_out[2 * g + i, :, pl.ds(h * HALF, HALF)] = keep_b[g, h, i] + recv_b[g, h, i]
        for i in (2 * g, 2 * g + 1):
            d = Y_ORDER[i]
            if d:
                y_copy[d] = remote(
                    y_out.at[i], y_in.at[d - 1], y_send.at[d - 1], y_recv.at[d - 1], at(z, lax.rem(y + d, NY), x, c)
                )

    def att_last():
        total = y_out[Y_ORDER.index(0)]
        for d in Y_ORDER:
            if d:
                y_copy[d].wait_recv()
                total = total + y_in[d - 1]
        att_ref[...] = total
        outs.append(pltpu.make_async_copy(att_ref, att_hbm, out_sem.at[0]))
        outs[-1].start()
        squares.append(squares_of(total))

    work = {"second": att_second, "third": att_third, "last": lambda g: att_last()}

    for n in range(PIECES):
        way, k = n % 2, n % 2 * SPLIT + n // 2
        exp_piece(k)
        if n == 0:
            pl.semaphore_wait(barrier, len(greeted))
        ring_start(way, k)
        if n == 1:
            att_group(0)
    for n in range(PIECES):
        way, k = n % 2, (1 - n % 2) * SPLIT + n // 2
        ring_start(way, k)
    for g in range(1, GROUPS):
        att_group(g)
    for g in range(GROUPS):
        att_first(g)
    event = 0
    for unit in range(2 * DEPTH - 1):
        hops = DEPTH - (unit + 1) // 2
        for p in range(SPLIT):
            for way in range(2):
                half = way if unit % 2 == 0 else 1 - way
                ring_step(way, half * SPLIT + p, hops)
            for name, g in BETWEEN.get(event * 2 // SPLIT, ()) if event * 2 % SPLIT == 0 else ():
                work[name](g)
            event += 1

    value = squares[0]
    for other in squares[1:]:
        value = value + other
    norm_c[...] = jnp.sum(value, axis=0, keepdims=True)

    def norm_copy(n, src, dst, device):
        return pltpu.make_async_remote_copy(
            src_ref=src, dst_ref=dst, send_sem=norm_send.at[n], recv_sem=norm_recv.at[n],
            device_id=device, device_id_type=MESH,
        )

    for d in (4, 3, 5, 2, 6, 1, 7):
        norm_copy(0, norm_c, norm_z.at[d * NC + c], at(lax.rem(z + d, NZ), y, x, 1)).start()

    @pl.when(c == 0)
    def _():
        norm_copy(0, norm_c, norm_z.at[0], at(z, y, x, 1)).start()

    for copy in sends:
        copy.wait_send()
    for out in outs:
        out.wait()

    @pl.when(c == 0)
    def _():
        sent = norm_z.at[pl.ds(0, NZ)]
        pltpu.make_async_copy(sent, sent, norm_send.at[0]).wait()
        pltpu.make_async_copy(norm_p, norm_p, norm_recv.at[1]).wait()

    @pl.when(c == 1)
    def _():
        norm_z[1] = norm_c[...]
        others = norm_z.at[pl.ds(0, NZ * NC - 1)]
        pltpu.make_async_copy(others, others, norm_recv.at[0]).wait()
        norm_p[0] = jnp.sum(norm_z[...], axis=0)
        plane = [(dy, dx) for dy in range(NY) for dx in range(NX) if dy or dx]
        plane.sort(key=lambda e: -min(e[0], NY - e[0]) - min(e[1], NX - e[1]))
        for core in range(NC):
            for dy, dx in plane if core else plane + [(0, 0)]:
                device = at(z, lax.rem(y + dy, NY), lax.rem(x + dx, NX), core)
                norm_copy(1, norm_p.at[0], norm_p.at[dy * NX + dx], device).start()
        sent = norm_z.at[pl.ds(0, NZ - 1)]
        pltpu.make_async_copy(sent, sent, norm_send.at[0]).wait()
        others = norm_p.at[pl.ds(1, NX * NY - 1)]
        pltpu.make_async_copy(others, others, norm_recv.at[1]).wait()
        for sent in (norm_p, others):
            pltpu.make_async_copy(sent, sent, norm_send.at[1]).wait()

    norm_ref[...] = jnp.sum(norm_p[...], axis=0)


def grads(hidden, cot, kv, xin, counts):
    f32, bf16 = jnp.float32, jnp.bfloat16
    dma = pltpu.SemaphoreType.DMA
    hbm = pl.BlockSpec(memory_space=pltpu.HBM)
    vmem = pl.BlockSpec(memory_space=pltpu.VMEM)
    return pl.pallas_call(
        grads_kernel,
        out_shape=tuple(jax.ShapeDtypeStruct(shape, f32) for shape in ((OWN, DW), (ROWS, COLS), (1, 128))),
        in_specs=[hbm] * 5,
        out_specs=(hbm, hbm, vmem),
        scratch_shapes=[
            pltpu.VMEM((OWN, DW), f32),
            pltpu.VMEM((ROWS, COLS), f32),
            pltpu.SMEM((1, 1), jnp.int32),
            pltpu.VMEM((HID, TOK), bf16),
            pltpu.VMEM((PIECES, TOK, WIDE), bf16),
            pltpu.VMEM((TOK, KV2), bf16),
            pltpu.VMEM((TOK, COLS), bf16),
            pltpu.VMEM((HID, TOK), bf16),
            pltpu.VMEM((PIECES, NZ, OWN, WIDE), f32),
            pltpu.VMEM((2, PIECES, DEPTH, OWN, WIDE), f32),
            pltpu.VMEM((NY, NX, NC, ROWS, COLS), f32),
            pltpu.VMEM((GROUPS, 2, NX, ROWS, COLS), f32),
            pltpu.VMEM((GROUPS, 2, 2, 2, ROWS, HALF), f32),
            pltpu.VMEM((GROUPS, 2, 2, 2, ROWS, HALF), f32),
            pltpu.VMEM((GROUPS, 2, 2, 2, ROWS, HALF), f32),
            pltpu.VMEM((GROUPS, 2, 2, ROWS, HALF), f32),
            pltpu.VMEM((GROUPS, 2, 2, ROWS, HALF), f32),
            pltpu.VMEM((GROUPS, 2, 2, ROWS, HALF), f32),
            pltpu.VMEM((NY, ROWS, COLS), f32),
            pltpu.VMEM((NY - 1, ROWS, COLS), f32),
            pltpu.VMEM((1, 128), f32),
            pltpu.VMEM((NZ * NC, 1, 128), f32),
            pltpu.VMEM((NX * NY, 1, 128), f32),
            dma((4 + PIECES,)),
            dma((2, PIECES, DEPTH)),
            dma((2, PIECES, DEPTH)),
            dma((GROUPS,)),
            dma((GROUPS,)),
            dma((GROUPS, 2)),
            dma((GROUPS, 2)),
            dma((GROUPS, 2)),
            dma((GROUPS, 2)),
            dma((NY - 1,)),
            dma((NY - 1,)),
            dma((2,)),
            dma((2,)),
            dma((1 + PIECES,)),
        ],
        compiler_params=pltpu.CompilerParams(
            collective_id=0, has_side_effects=True, vmem_limit_bytes=60 * 1024 * 1024
        ),
        name="grads",
    )(hidden, cot, kv, xin, counts)


BLOCKS = 4


def update_kernel(norm_hbm, *refs):
    att_in, exp_in, att_out, exp_out = refs[0:4], refs[4:8], refs[8:11], refs[11:14]
    norm, att, exp, new_att, new_exp, load_sem, store_sem = refs[14:]
    wide = DW // BLOCKS
    cols = [pl.ds(n * wide, wide) for n in range(BLOCKS)]
    loads = [[pltpu.make_async_copy(norm_hbm, norm, load_sem.at[0, 4])]]
    loads[0] += [pltpu.make_async_copy(a, att.at[i], load_sem.at[0, i]) for i, a in enumerate(att_in)]
    for n in range(BLOCKS):
        loads.append(
            [pltpu.make_async_copy(a.at[:, cols[n]], exp.at[i, :, cols[n]], load_sem.at[1 + n, i]) for i, a in enumerate(exp_in)]
        )
    for part in loads:
        for load in part:
            load.start()
    stores = []

    def block(n, values, keep, sources, targets):
        new = adam_update(*values, clip)
        for i in range(3):
            keep(i, new[i])
            stores.append(pltpu.make_async_copy(sources[i], targets[i], store_sem.at[n, i]))
            stores[-1].start()

    for load in loads[0]:
        load.wait()
    entries = float(KV2 * D + NY * NX * NC // GROUP * FF * DW)
    square_sum = jnp.sum(norm[...], axis=1, keepdims=True)
    clip = jnp.minimum(1.0, jnp.sqrt(jnp.full_like(square_sum, entries)) / (jnp.sqrt(square_sum) + 1e-06))

    def keep_att(i, value):
        new_att[i] = value

    block(0, [att[i] for i in range(4)], keep_att, [new_att.at[i] for i in range(3)], att_out)
    for n in range(BLOCKS):
        for load in loads[1 + n]:
            load.wait()

        def keep_exp(i, value):
            new_exp[i, :, cols[n]] = value

        block(
            1 + n,
            [exp[i, :, cols[n]] for i in range(4)],
            keep_exp,
            [new_exp.at[i, :, cols[n]] for i in range(3)],
            [ref.at[:, cols[n]] for ref in exp_out],
        )
    for store in stores:
        store.wait()


def update(norm, att, exp):
    f32 = jnp.float32
    hbm = pl.BlockSpec(memory_space=pltpu.HBM)
    return pl.pallas_call(
        update_kernel,
        out_shape=tuple(jax.ShapeDtypeStruct(a.shape, f32) for a in (*att[:3], *exp[:3])),
        in_specs=[hbm] * 9,
        out_specs=(hbm,) * 6,
        scratch_shapes=[
            pltpu.VMEM((1, 128), f32),
            pltpu.VMEM((4, ROWS, COLS), f32),
            pltpu.VMEM((4, OWN, DW), f32),
            pltpu.VMEM((3, ROWS, COLS), f32),
            pltpu.VMEM((3, OWN, DW), f32),
            pltpu.SemaphoreType.DMA((1 + BLOCKS, 5)),
            pltpu.SemaphoreType.DMA((1 + BLOCKS, 3)),
        ],
        compiler_params=pltpu.CompilerParams(vmem_limit_bytes=60 * 1024 * 1024),
        name="update",
    )(norm, *att, *exp)


def on_device(
    att_input,
    kv_cotangent,
    expert_hidden,
    expert_cotangent,
    token_counts,
    att_param,
    att_moment,
    att_second,
    exp_param,
    exp_moment,
    exp_second,
):
    exp_grad, att_grad, norm = grads(expert_hidden.T, expert_cotangent, kv_cotangent, att_input, token_counts)
    return update(
        norm,
        (att_param, att_moment, att_second, att_grad),
        (exp_param, exp_moment, exp_second, exp_grad),
    )


def solution(mesh):
    in_specs = (
        P("dp", "expert"),
        P("dp", None),
        P("expert", "dp"),
        P("expert", "dp"),
        P("dp", "expert"),
        P("dp", "expert"),
        P("dp", "expert"),
        P("dp", "expert"),
        P(("dp", "expert"), None),
        P(("dp", "expert"), None),
        P(("dp", "expert"), None),
    )
    out_specs = (
        P("dp", "expert"),
        P("dp", "expert"),
        P("dp", "expert"),
        P(("dp", "expert"), None),
        P(("dp", "expert"), None),
        P(("dp", "expert"), None),
    )
    return jax.shard_map(
        on_device, mesh=mesh, in_specs=in_specs, out_specs=out_specs, check_vma=False
    )
```

time: 63.7 us -> 49.1 us (0.77)
  Pallas kernels: 55.8 us -> 47.6 us
  local copies, waits for them, and re-layouts: 6.36 us -> 0 us
    pallas_call x2, Pallas kernels: 55.8 us -> 47.6 us  [the longest x1 45.4 us: grads(): pl.pallas_call(grads_kernel, out_shape=tuple((jax.ShapeDtypeStruct(shape,...]
    unnamed x13 -> x0, local copies, waits for them, and re-layouts: 6.36 us -> none
where the time goes in v2:
time: 49.1 us; the launch traced here: 48.9 us
  Pallas kernels  47.6 us (97%)
  between operations  1.29 us (3%)
    pallas_call x1, Pallas kernels, grads(): pl.pallas_call(grads_kernel, out_shape=tuple((jax.ShapeDtypeStruct(shape,...  45.4 us
    pallas_call x1, Pallas kernels, update(): pl.pallas_call(update_kernel, out_shape=tuple((jax.ShapeDtypeStruct(a.sha...  2.25 us

profile of v2, /device:TPU:1, one launch (start us, length us, event | category | flops | bytes accessed | tf_op | source)
XLA Modules:
  0.0 48.9 jit_solution(5128490329015366559)
XLA Ops:
  1.3 45.4 %grads.1 = (f32[24,2048]{1,0:T(8,128)}, f32[16,512]{1,0:T(8,128)}, f32[1,128]{1,0:T(1,128)}) custom-call(bf16[192,384]{1,0:T(8,128)(2,1)} %bitcast.1, bf16[384,2048]{1,0:T(8,128)(2,1)} %cot_hbm.1, bf16[384,1024]{1,0:T(8,128)(2,1)} %kv_hbm.1, bf16[384,512]{1,0:T(8,128)(2,1)} %x_hbm.1, s32[1,1]{1,0:T(1,128)S(6)} %copy.17.count_hbm), custom_call_target="tpu_custom_call" | custom-call | tf_op jit(solution)/shard_map/grads/pallas_call | solution.py:318
  46.7 2.2 %update.1 = (f32[16,512]{1,0:T(8,128)}, f32[16,512]{1,0:T(8,128)}, f32[16,512]{1,0:T(8,128)}, f32[24,2048]{1,0:T(8,128)}, f32[24,2048]{1,0:T(8,128)}, /*index=5*/f32[24,2048]{1,0:T(8,128)}) custom-call(f32[1,128]{1,0:T(1,128)} %get-tuple-element.9.norm_hbm, f32[16,512]{1,0:T(8,128)} %refs_0_.1, f32[16,512]{1,0:T(8,128)} %refs_1_.1, f32[16,512]{1,0:T(8,128)} %refs_2_.1, ...), custom_call_target="tpu_custom_call" | custom-call | tf_op jit(solution)/shard_map/update/pallas_call | solution.py:426

commit v3 on v2

--- a/solution.py
+++ b/solution.py
@@ -29,21 +29,27 @@
 PIECES = HALVES * SPLIT
 WIDE = DW // PIECES
 DEPTH = NZ // 2
+SLOTS = {}
+for _way in range(2):
+    for _piece in range(PIECES):
+        for _hops in range(1, DEPTH + (_piece // SPLIT == _way)):
+            SLOTS[_way, _piece, _hops] = len(SLOTS)
 COLS = 512
 HALF = COLS // 2
 ROWS = 16
 GROUPS = 4
 Y_ORDER = (4, 3, 5, 2, 6, 1, 7, 0)
 MESH = pl.DeviceIdType.MESH
+RING, ATT, NORM = True, True, True
 BETWEEN = {
-    3: (("second", 0),),
-    5: (("second", 1),),
-    6: (("second", 2),),
-    8: (("second", 3), ("third", 0)),
-    9: (("third", 1),),
-    10: (("third", 2),),
-    11: (("third", 3),),
-    12: (("last", 0),),
+    1: (('second', 0),),
+    2: (('second', 1),),
+    3: (('second', 2),),
+    5: (('second', 3), ('third', 0)),
+    6: (('third', 1),),
+    7: (('third', 2),),
+    8: (('third', 3),),
+    11: (('last', 0),),
 }
 
 
@@ -103,14 +109,14 @@
                     total = total + value[i : i + 8, j : j + 128]
         return total
 
-    sends = []
+    def arrived(ref, sem):
+        pltpu.make_async_copy(ref, ref, sem).wait()
 
     def remote(src, dst, send_sem, recv_sem, device):
         copy = pltpu.make_async_remote_copy(
             src_ref=src, dst_ref=dst, send_sem=send_sem, recv_sem=recv_sem, device_id=device, device_id_type=MESH
         )
         copy.start()
-        sends.append(copy)
         return copy
 
     towards = (at(lax.rem(z + NZ - 1, NZ), y, x, c), at(lax.rem(z + 1, NZ), y, x, c))
@@ -121,31 +127,35 @@
     arrivals = {}
 
     def ring_send_step(way, k, hops, src):
-        arrivals[way, k, hops] = remote(
-            src, ring.at[way, k, hops - 1], ring_send.at[way, k, hops - 1], ring_recv.at[way, k, hops - 1], towards[way]
-        )
+        if not RING:
+            return
+        slot = SLOTS[way, k, hops]
+        arrivals[way, k, hops] = remote(src, ring.at[slot], ring_send.at[0], ring_recv.at[slot], towards[way])
 
     def ring_start(way, k):
+        if not RING:
+            return
         hops = DEPTH if k // SPLIT == way else DEPTH - 1
         ring_send_step(way, k, hops, part.at[k, shard(way, hops)])
 
-    squares, outs = [], []
+    squares = []
 
     def ring_step(way, k, hops):
-        arrivals[way, k, hops].wait_recv()
+        if RING:
+            arrivals[way, k, hops].wait_recv()
         left = hops - 1
+        slot = SLOTS[way, k, hops]
         if left:
-            ring[way, k, left] = ring[way, k, left] + part[k, shard(way, left)]
-            ring_send_step(way, k, left, ring.at[way, k, left])
+            ring[slot] = ring[slot] + part[k, shard(way, left)]
+            ring_send_step(way, k, left, ring.at[slot])
             return
         cols = pl.ds(k % PIECES * WIDE, WIDE)
         if k // SPLIT != way:
-            exp_ref[:, cols] = part[k, z] + ring[way, k, 0]
+            exp_ref[:, cols] = part[k, z] + ring[slot]
         else:
-            total = exp_ref[:, cols] + ring[way, k, 0]
+            total = exp_ref[:, cols] + ring[slot]
             exp_ref[:, cols] = total
-            outs.append(pltpu.make_async_copy(exp_ref.at[:, cols], exp_hbm.at[:, cols], out_sem.at[1 + k]))
-            outs[-1].start()
+            pltpu.make_async_copy(exp_ref.at[:, cols], exp_hbm.at[:, cols], out_sem.at[0]).start()
             squares.append(squares_of(total))
 
     count_load.wait()
@@ -160,9 +170,11 @@
         )
         part[k] = block.reshape(NZ, OWN, WIDE)
 
-    core_copy, a_copy, b_copy = {}, {}, {}
+    core_copy = {}
 
     def att_group(g):
+        if not ATT:
+            return
         if g == 0:
             loads[1 + PIECES].wait()
             loads[2 + PIECES].wait()
@@ -172,7 +184,7 @@
             block = lax.dot_general(columns, xin[...], (((0,), (0,)), ((), ())), preferred_element_type=jnp.float32)
             grad[i] = block.reshape(NX, NC, ROWS, COLS)
         core_copy[g] = remote(
-            grad.at[pl.ds(2 * g, 2), :, 1 - c], core_in.at[g], core_send.at[g], core_recv.at[g], at(z, y, x, 1 - c)
+            grad.at[pl.ds(2 * g, 2), :, 1 - c], core_in.at[g], core_send.at[0], core_recv.at[g], at(z, y, x, 1 - c)
         )
 
     slots = ((0, 3, 1, 2), (0, 1, 3, 2))
@@ -180,6 +192,8 @@
     second_to = (x_rel[3], x_rel[1])
 
     def att_first(g):
+        if not ATT:
+            return
         core_copy[g].wait_recv()
         for h in range(2):
             cols = pl.ds(h * HALF, HALF)
@@ -187,8 +201,8 @@
                 at_x = x_rel[slots[h][j]]
                 for i in range(2):
                     send_a[g, h, j - 2, i] = grad[2 * g + i, at_x, c, :, cols] + core_in[g, i, at_x, :, cols]
-            a_copy[g, h] = remote(
-                send_a.at[g, h], recv_a.at[g, h], a_send.at[g, h], a_recv.at[g, h], at(z, y, first_to[h], c)
+            remote(
+                send_a.at[g, h], recv_a.at[g, h], a_send.at[0], a_recv.at[g], at(z, y, first_to[h], c)
             )
         for h in range(2):
             cols = pl.ds(h * HALF, HALF)
@@ -198,37 +212,40 @@
                     keep[g, h, j, i] = grad[2 * g + i, at_x, c, :, cols] + core_in[g, i, at_x, :, cols]
 
     def att_second(g):
+        if not ATT:
+            return
+        arrived(recv_a.at[g], a_recv.at[g])
         for h in range(2):
-            a_copy[g, h].wait_recv()
             send_b[g, h] = keep[g, h, 1] + recv_a[g, h, 1]
-            b_copy[g, h] = remote(
-                send_b.at[g, h], recv_b.at[g, h], b_send.at[g, h], b_recv.at[g, h], at(z, y, second_to[h], c)
+            remote(
+                send_b.at[g, h], recv_b.at[g, h], b_send.at[0], b_recv.at[g], at(z, y, second_to[h], c)
             )
             keep_b[g, h] = keep[g, h, 0] + recv_a[g, h, 0]
 
-    y_copy = {}
-
     def att_third(g):
+        if not ATT:
+            return
+        arrived(recv_b.at[g], b_recv.at[g])
         for h in range(2):
-            b_copy[g, h].wait_recv()
             for i in range(2):
                 y_out[2 * g + i, :, pl.ds(h * HALF, HALF)] = keep_b[g, h, i] + recv_b[g, h, i]
         for i in (2 * g, 2 * g + 1):
             d = Y_ORDER[i]
             if d:
-                y_copy[d] = remote(
-                    y_out.at[i], y_in.at[d - 1], y_send.at[d - 1], y_recv.at[d - 1], at(z, lax.rem(y + d, NY), x, c)
+                remote(
+                    y_out.at[i], y_in.at[d - 1], y_send.at[0], y_recv.at[0], at(z, lax.rem(y + d, NY), x, c)
                 )
 
     def att_last():
+        if not ATT:
+            return
+        arrived(y_in, y_recv.at[0])
         total = y_out[Y_ORDER.index(0)]
         for d in Y_ORDER:
             if d:
-                y_copy[d].wait_recv()
                 total = total + y_in[d - 1]
         att_ref[...] = total
-        outs.append(pltpu.make_async_copy(att_ref, att_hbm, out_sem.at[0]))
-        outs[-1].start()
+        pltpu.make_async_copy(att_ref, att_hbm, out_sem.at[1]).start()
         squares.append(squares_of(total))
 
     work = {"second": att_second, "third": att_third, "last": lambda g: att_last()}
@@ -277,10 +294,11 @@
     def _():
         norm_copy(0, norm_c, norm_z.at[0], at(z, y, x, 1)).start()
 
-    for copy in sends:
-        copy.wait_send()
-    for out in outs:
-        out.wait()
+    for ref, sem in (
+        (ring, ring_send), (core_in, core_send), (send_a, a_send), (send_b, b_send), (y_in, y_send), (exp_ref, out_sem)
+    ):
+        arrived(ref, sem.at[0])
+    arrived(att_ref, out_sem.at[1])
 
     @pl.when(c == 0)
     def _():
@@ -330,7 +348,7 @@
             pltpu.VMEM((TOK, COLS), bf16),
             pltpu.VMEM((HID, TOK), bf16),
             pltpu.VMEM((PIECES, NZ, OWN, WIDE), f32),
-            pltpu.VMEM((2, PIECES, DEPTH, OWN, WIDE), f32),
+            pltpu.VMEM((len(SLOTS), OWN, WIDE), f32),
             pltpu.VMEM((NY, NX, NC, ROWS, COLS), f32),
             pltpu.VMEM((GROUPS, 2, NX, ROWS, COLS), f32),
             pltpu.VMEM((GROUPS, 2, 2, 2, ROWS, HALF), f32),
@@ -345,22 +363,22 @@
             pltpu.VMEM((NZ * NC, 1, 128), f32),
             pltpu.VMEM((NX * NY, 1, 128), f32),
             dma((4 + PIECES,)),
-            dma((2, PIECES, DEPTH)),
-            dma((2, PIECES, DEPTH)),
+            dma((1,)),
+            dma((len(SLOTS),)),
+            dma((1,)),
             dma((GROUPS,)),
+            dma((1,)),
             dma((GROUPS,)),
-            dma((GROUPS, 2)),
-            dma((GROUPS, 2)),
-            dma((GROUPS, 2)),
-            dma((GROUPS, 2)),
-            dma((NY - 1,)),
-            dma((NY - 1,)),
+            dma((1,)),
+            dma((GROUPS,)),
+            dma((1,)),
+            dma((1,)),
             dma((2,)),
             dma((2,)),
-            dma((1 + PIECES,)),
+            dma((2,)),
         ],
         compiler_params=pltpu.CompilerParams(
-            collective_id=0, has_side_effects=True, vmem_limit_bytes=60 * 1024 * 1024
+            collective_id=0, has_side_effects=True, vmem_limit_bytes=55091 * 1024
         ),
         name="grads",
     )(hidden, cot, kv, xin, counts)
@@ -374,26 +392,24 @@
     norm, att, exp, new_att, new_exp, load_sem, store_sem = refs[14:]
     wide = DW // BLOCKS
     cols = [pl.ds(n * wide, wide) for n in range(BLOCKS)]
-    loads = [[pltpu.make_async_copy(norm_hbm, norm, load_sem.at[0, 4])]]
-    loads[0] += [pltpu.make_async_copy(a, att.at[i], load_sem.at[0, i]) for i, a in enumerate(att_in)]
+    pltpu.make_async_copy(norm_hbm, norm, load_sem.at[0]).start()
+    for i, a in enumerate(att_in):
+        pltpu.make_async_copy(a, att.at[i], load_sem.at[1]).start()
     for n in range(BLOCKS):
-        loads.append(
-            [pltpu.make_async_copy(a.at[:, cols[n]], exp.at[i, :, cols[n]], load_sem.at[1 + n, i]) for i, a in enumerate(exp_in)]
-        )
-    for part in loads:
-        for load in part:
-            load.start()
-    stores = []
-
-    def block(n, values, keep, sources, targets):
+        for i, a in enumerate(exp_in):
+            pltpu.make_async_copy(a.at[:, cols[n]], exp.at[i, :, cols[n]], load_sem.at[2 + n]).start()
+
+    def arrived(ref, sem):
+        pltpu.make_async_copy(ref, ref, sem).wait()
+
+    def block(values, keep, sources, targets, sem):
         new = adam_update(*values, clip)
         for i in range(3):
             keep(i, new[i])
-            stores.append(pltpu.make_async_copy(sources[i], targets[i], store_sem.at[n, i]))
-            stores[-1].start()
-
-    for load in loads[0]:
-        load.wait()
+            pltpu.make_async_copy(sources[i], targets[i], sem).start()
+
+    arrived(norm, load_sem.at[0])
+    arrived(att, load_sem.at[1])
     entries = float(KV2 * D + NY * NX * NC // GROUP * FF * DW)
     square_sum = jnp.sum(norm[...], axis=1, keepdims=True)
     clip = jnp.minimum(1.0, jnp.sqrt(jnp.full_like(square_sum, entries)) / (jnp.sqrt(square_sum) + 1e-06))
@@ -401,23 +417,22 @@
     def keep_att(i, value):
         new_att[i] = value
 
-    block(0, [att[i] for i in range(4)], keep_att, [new_att.at[i] for i in range(3)], att_out)
+    block([att[i] for i in range(4)], keep_att, [new_att.at[i] for i in range(3)], att_out, store_sem.at[0])
     for n in range(BLOCKS):
-        for load in loads[1 + n]:
-            load.wait()
+        arrived(exp.at[:, :, cols[n]], load_sem.at[2 + n])
 
         def keep_exp(i, value):
             new_exp[i, :, cols[n]] = value
 
         block(
-            1 + n,
             [exp[i, :, cols[n]] for i in range(4)],
             keep_exp,
             [new_exp.at[i, :, cols[n]] for i in range(3)],
             [ref.at[:, cols[n]] for ref in exp_out],
+            store_sem.at[1],
         )
-    for store in stores:
-        store.wait()
+    arrived(new_att, store_sem.at[0])
+    arrived(new_exp, store_sem.at[1])
 
 
 def update(norm, att, exp):
@@ -434,10 +449,10 @@
             pltpu.VMEM((4, OWN, DW), f32),
             pltpu.VMEM((3, ROWS, COLS), f32),
             pltpu.VMEM((3, OWN, DW), f32),
-            pltpu.SemaphoreType.DMA((1 + BLOCKS, 5)),
-            pltpu.SemaphoreType.DMA((1 + BLOCKS, 3)),
+            pltpu.SemaphoreType.DMA((2 + BLOCKS,)),
+            pltpu.SemaphoreType.DMA((2,)),
         ],
-        compiler_params=pltpu.CompilerParams(vmem_limit_bytes=60 * 1024 * 1024),
+        compiler_params=pltpu.CompilerParams(vmem_limit_bytes=55091 * 1024),
         name="update",
     )(norm, *att, *exp)
 

time: 49.1 us -> 46.4 us (0.945)
  Pallas kernels: 47.6 us -> 44.7 us
    pallas_call x1, Pallas kernels: 45.4 us -> 42.6 us  [grads(): pl.pallas_call(grads_kernel, out_shape=tuple((jax.ShapeDtypeStruct(shape,...]
where the time goes in v3:
time: 46.4 us; the launch traced here: 46.1 us
  Pallas kernels  44.7 us (96%)
  between operations  1.35 us (3%)
    pallas_call x1, Pallas kernels, grads(): pl.pallas_call(grads_kernel, out_shape=tuple((jax.ShapeDtypeStruct(shape,...  42.6 us
    pallas_call x1, Pallas kernels, update(): pl.pallas_call(update_kernel, out_shape=tuple((jax.ShapeDtypeStruct(a.sha...  2.11 us

profile of v3, /device:TPU:1, one launch (start us, length us, event | category | flops | bytes accessed | tf_op | source)
XLA Modules:
  0.0 46.1 jit_solution(1282624763832734542)
XLA Ops:
  0.6 0.0 copy-start.2
  0.6 0.0 copy-start.1
  0.7 0.0 copy-start
  1.3 42.6 %grads.1 = (f32[24,2048]{1,0:T(8,128)}, f32[16,512]{1,0:T(8,128)S(1)}, f32[1,128]{1,0:T(1,128)S(1)}) custom-call(bf16[192,384]{1,0:T(8,128)(2,1)} %bitcast.1, bf16[384,2048]{1,0:T(8,128)(2,1)} %cot_hbm.1, bf16[384,1024]{1,0:T(8,128)(2,1)} %kv_hbm.1, bf16[384,512]{1,0:T(8,128)(2,1)} %x_hbm.1, s32[1,1]{1,0:T(1,128)S(6)} %copy.17.count_hbm), custom_call_target="tpu_custom_call" | custom-call | tf_op jit(solution)/shard_map/grads/pallas_call | solution.py:336
  43.9 0.0 copy-done.2
  43.9 0.0 copy-done.1
  44.0 0.0 copy-done
  44.0 2.1 %update.1 = (f32[16,512]{1,0:T(8,128)}, f32[16,512]{1,0:T(8,128)}, f32[16,512]{1,0:T(8,128)}, f32[24,2048]{1,0:T(8,128)}, f32[24,2048]{1,0:T(8,128)}, /*index=5*/f32[24,2048]{1,0:T(8,128)}) custom-call(f32[1,128]{1,0:T(1,128)S(1)} %get-tuple-element.9.norm_hbm, f32[16,512]{1,0:T(8,128)S(1)} %copy-done, f32[16,512]{1,0:T(8,128)S(1)} %copy-done.1, ...), custom_call_target="tpu_custom_call" | custom-call | tf_op jit(solution)/shard_map/update/pallas_call | solution.py:441
Async XLA Ops:
  0.6 43.3 %copy-start.2 = (f32[16,512]{1,0:T(8,128)S(1)}, f32[16,512]{1,0:T(8,128)}, u32[]{:S(2)}) copy-start(f32[16,512]{1,0:T(8,128)} %refs_2_.1) | copy-start | bytes 98308
  0.6 43.3 %copy-start.1 = (f32[16,512]{1,0:T(8,128)S(1)}, f32[16,512]{1,0:T(8,128)}, u32[]{:S(2)}) copy-start(f32[16,512]{1,0:T(8,128)} %refs_1_.1) | copy-start | bytes 98308
  0.7 43.3 %copy-start = (f32[16,512]{1,0:T(8,128)S(1)}, f32[16,512]{1,0:T(8,128)}, u32[]{:S(2)}) copy-start(f32[16,512]{1,0:T(8,128)} %refs_0_.1) | copy-start | bytes 98308

commit v4 on v3

--- a/solution.py
+++ b/solution.py
@@ -29,11 +29,12 @@
 PIECES = HALVES * SPLIT
 WIDE = DW // PIECES
 DEPTH = NZ // 2
-SLOTS = {}
-for _way in range(2):
-    for _piece in range(PIECES):
-        for _hops in range(1, DEPTH + (_piece // SPLIT == _way)):
-            SLOTS[_way, _piece, _hops] = len(SLOTS)
+STEPS = [
+    (DEPTH - (unit + 1) // 2, unit % 2 * SPLIT + p, (1 - unit % 2) * SPLIT + p)
+    for unit in range(2 * DEPTH - 1)
+    for p in range(SPLIT)
+]
+SLOTS = {(way, step[1 + way], step[0]): (n, way) for n, step in enumerate(STEPS) for way in range(2)}
 COLS = 512
 HALF = COLS // 2
 ROWS = 16
@@ -96,8 +97,8 @@
     loads.append(pltpu.make_async_copy(kv_hbm, kv, load_sem.at[2 + PIECES]))
     count_load = pltpu.make_async_copy(count_hbm, count_ref, load_sem.at[3 + PIECES])
     count_load.start()
-    for load in loads:
-        load.start()
+    for n in (1 + PIECES, 2 + PIECES, *range(1 + PIECES)):
+        loads[n].start()
 
     def squares_of(value):
         rows, width = value.shape
@@ -124,13 +125,11 @@
     def shard(way, hops):
         return lax.rem(z + NZ - hops, NZ) if way == 0 else lax.rem(z + hops, NZ)
 
-    arrivals = {}
-
     def ring_send_step(way, k, hops, src):
         if not RING:
             return
-        slot = SLOTS[way, k, hops]
-        arrivals[way, k, hops] = remote(src, ring.at[slot], ring_send.at[0], ring_recv.at[slot], towards[way])
+        n, _ = SLOTS[way, k, hops]
+        remote(src, ring.at[n, way], ring_send.at[0], ring_recv.at[n], towards[way])
 
     def ring_start(way, k):
         if not RING:
@@ -140,23 +139,23 @@
 
     squares = []
 
-    def ring_step(way, k, hops):
-        if RING:
-            arrivals[way, k, hops].wait_recv()
+    def ring_step(n):
+        hops, down, up = STEPS[n]
         left = hops - 1
-        slot = SLOTS[way, k, hops]
-        if left:
-            ring[slot] = ring[slot] + part[k, shard(way, left)]
-            ring_send_step(way, k, left, ring.at[slot])
-            return
-        cols = pl.ds(k % PIECES * WIDE, WIDE)
-        if k // SPLIT != way:
-            exp_ref[:, cols] = part[k, z] + ring[slot]
-        else:
-            total = exp_ref[:, cols] + ring[slot]
-            exp_ref[:, cols] = total
-            pltpu.make_async_copy(exp_ref.at[:, cols], exp_hbm.at[:, cols], out_sem.at[0]).start()
-            squares.append(squares_of(total))
+        arrived(ring.at[n], ring_recv.at[n])
+        for way, k in enumerate((down, up)):
+            if left:
+                ring[n, way] = ring[n, way] + part[k, shard(way, left)]
+                ring_send_step(way, k, left, ring.at[n, way])
+                continue
+            cols = pl.ds(k * WIDE, WIDE)
+            if k // SPLIT != way:
+                exp_ref[:, cols] = part[k, z] + ring[n, way]
+            else:
+                total = exp_ref[:, cols] + ring[n, way]
+                exp_ref[:, cols] = total
+                pltpu.make_async_copy(exp_ref.at[:, cols], exp_hbm.at[:, cols], out_sem.at[0]).start()
+                squares.append(squares_of(total))
 
     count_load.wait()
     loads[0].wait()
@@ -250,31 +249,29 @@
 
     work = {"second": att_second, "third": att_third, "last": lambda g: att_last()}
 
-    for n in range(PIECES):
-        way, k = n % 2, n % 2 * SPLIT + n // 2
-        exp_piece(k)
-        if n == 0:
-            pl.semaphore_wait(barrier, len(greeted))
-        ring_start(way, k)
-        if n == 1:
-            att_group(0)
-    for n in range(PIECES):
-        way, k = n % 2, (1 - n % 2) * SPLIT + n // 2
-        ring_start(way, k)
-    for g in range(1, GROUPS):
-        att_group(g)
+    pl.semaphore_wait(barrier, len(greeted))
+    att_group(0)
+    att_group(1)
+    exp_piece(0)
+    ring_start(0, 0)
+    exp_piece(2)
+    ring_start(1, 2)
+    exp_piece(1)
+    ring_start(0, 1)
+    exp_piece(3)
+    ring_start(1, 3)
+    ring_start(0, 2)
+    ring_start(1, 0)
+    ring_start(0, 3)
+    ring_start(1, 1)
+    att_group(2)
+    att_group(3)
     for g in range(GROUPS):
         att_first(g)
-    event = 0
-    for unit in range(2 * DEPTH - 1):
-        hops = DEPTH - (unit + 1) // 2
-        for p in range(SPLIT):
-            for way in range(2):
-                half = way if unit % 2 == 0 else 1 - way
-                ring_step(way, half * SPLIT + p, hops)
-            for name, g in BETWEEN.get(event * 2 // SPLIT, ()) if event * 2 % SPLIT == 0 else ():
-                work[name](g)
-            event += 1
+    for n in range(len(STEPS)):
+        ring_step(n)
+        for name, g in BETWEEN.get(n, ()):
+            work[name](g)
 
     value = squares[0]
     for other in squares[1:]:
@@ -348,7 +345,7 @@
             pltpu.VMEM((TOK, COLS), bf16),
             pltpu.VMEM((HID, TOK), bf16),
             pltpu.VMEM((PIECES, NZ, OWN, WIDE), f32),
-            pltpu.VMEM((len(SLOTS), OWN, WIDE), f32),
+            pltpu.VMEM((len(STEPS), 2, OWN, WIDE), f32),
             pltpu.VMEM((NY, NX, NC, ROWS, COLS), f32),
             pltpu.VMEM((GROUPS, 2, NX, ROWS, COLS), f32),
             pltpu.VMEM((GROUPS, 2, 2, 2, ROWS, HALF), f32),
@@ -364,7 +361,7 @@
             pltpu.VMEM((NX * NY, 1, 128), f32),
             dma((4 + PIECES,)),
             dma((1,)),
-            dma((len(SLOTS),)),
+            dma((len(STEPS),)),
             dma((1,)),
             dma((GROUPS,)),
             dma((1,)),

time: 46.4 us -> 45.8 us (0.987)
  Pallas kernels: 44.7 us -> 44.2 us
    pallas_call x1, Pallas kernels: 42.6 us -> 42 us  [grads(): pl.pallas_call(grads_kernel, out_shape=tuple((jax.ShapeDtypeStruct(shape,...]
where the time goes in v4:
time: 45.8 us; the launch traced here: 45.5 us
  Pallas kernels  44.2 us (97%)
  between operations  1.35 us (3%)
    pallas_call x1, Pallas kernels, grads(): pl.pallas_call(grads_kernel, out_shape=tuple((jax.ShapeDtypeStruct(shape,...  42 us
    pallas_call x1, Pallas kernels, update(): pl.pallas_call(update_kernel, out_shape=tuple((jax.ShapeDtypeStruct(a.sha...  2.11 us

profile of v4, /device:TPU:1, one launch (start us, length us, event | category | flops | bytes accessed | tf_op | source)
XLA Modules:
  0.0 45.5 jit_solution(17367069871693323516)
XLA Ops:
  0.6 0.0 copy-start.2
  0.6 0.0 copy-start.1
  0.7 0.0 copy-start
  1.3 42.0 %grads.1 = (f32[24,2048]{1,0:T(8,128)}, f32[16,512]{1,0:T(8,128)S(1)}, f32[1,128]{1,0:T(1,128)S(1)}) custom-call(bf16[192,384]{1,0:T(8,128)(2,1)} %bitcast.1, bf16[384,2048]{1,0:T(8,128)(2,1)} %cot_hbm.1, bf16[384,1024]{1,0:T(8,128)(2,1)} %kv_hbm.1, bf16[384,512]{1,0:T(8,128)(2,1)} %x_hbm.1, s32[1,1]{1,0:T(1,128)S(6)} %copy.17.count_hbm), custom_call_target="tpu_custom_call" | custom-call | tf_op jit(solution)/shard_map/grads/pallas_call | solution.py:333
  43.4 0.0 copy-done.2
  43.4 0.0 copy-done.1
  43.4 0.0 copy-done
  43.4 2.1 %update.1 = (f32[16,512]{1,0:T(8,128)}, f32[16,512]{1,0:T(8,128)}, f32[16,512]{1,0:T(8,128)}, f32[24,2048]{1,0:T(8,128)}, f32[24,2048]{1,0:T(8,128)}, /*index=5*/f32[24,2048]{1,0:T(8,128)}) custom-call(f32[1,128]{1,0:T(1,128)S(1)} %get-tuple-element.9.norm_hbm, f32[16,512]{1,0:T(8,128)S(1)} %copy-done, f32[16,512]{1,0:T(8,128)S(1)} %copy-done.1, ...), custom_call_target="tpu_custom_call" | custom-call | tf_op jit(solution)/shard_map/update/pallas_call | solution.py:438
Async XLA Ops:
  0.6 42.7 %copy-start.2 = (f32[16,512]{1,0:T(8,128)S(1)}, f32[16,512]{1,0:T(8,128)}, u32[]{:S(2)}) copy-start(f32[16,512]{1,0:T(8,128)} %refs_2_.1) | copy-start | bytes 98308
  0.6 42.7 %copy-start.1 = (f32[16,512]{1,0:T(8,128)S(1)}, f32[16,512]{1,0:T(8,128)}, u32[]{:S(2)}) copy-start(f32[16,512]{1,0:T(8,128)} %refs_1_.1) | copy-start | bytes 98308
  0.7 42.7 %copy-start = (f32[16,512]{1,0:T(8,128)S(1)}, f32[16,512]{1,0:T(8,128)}, u32[]{:S(2)}) copy-start(f32[16,512]{1,0:T(8,128)} %refs_0_.1) | copy-start | bytes 98308

commit v5 on v4

--- a/solution.py
+++ b/solution.py
@@ -36,8 +36,9 @@
 ]
 SLOTS = {(way, step[1 + way], step[0]): (n, way) for n, step in enumerate(STEPS) for way in range(2)}
 COLS = 512
-HALF = COLS // 2
+MAIN = COLS - 128
 ROWS = 16
+HALF = ROWS // 2
 GROUPS = 4
 Y_ORDER = (4, 3, 5, 2, 6, 1, 7, 0)
 MESH = pl.DeviceIdType.MESH
@@ -48,7 +49,7 @@
     3: (('second', 2),),
     5: (('second', 3), ('third', 0)),
     6: (('third', 1),),
-    7: (('third', 2),),
+    7: (('third', 2), ('cross', 0)),
     8: (('third', 3),),
     11: (('last', 0),),
 }
@@ -69,8 +70,9 @@
     hidden_hbm, cot_hbm, kv_hbm, x_hbm, count_hbm,
     exp_hbm, att_hbm, norm_ref,
     exp_ref, att_ref, count_ref, hidden, cot, kv, xin, masked, part, ring, grad, core_in, keep, send_a, recv_a, keep_b, send_b, recv_b, y_out, y_in,
+    side, side_in, cross, cross_in,
     norm_c, norm_z, norm_p,
-    load_sem, ring_send, ring_recv, core_send, core_recv, a_send, a_recv, b_send, b_recv, y_send, y_recv, norm_send, norm_recv, out_sem,
+    load_sem, ring_send, ring_recv, core_send, core_recv, a_send, a_recv, b_send, b_recv, y_send, y_recv, side_send, side_recv, cross_send, cross_recv, norm_send, norm_recv, out_sem,
 ):
     dp = lax.axis_index("dp")
     z = lax.axis_index("expert")
@@ -85,7 +87,7 @@
 
     barrier = pltpu.get_barrier_semaphore()
     greeted = [at(lax.rem(z + 1, NZ), y, x, c), at(lax.rem(z + NZ - 1, NZ), y, x, c), at(z, y, x, 1 - c)]
-    greeted += [at(z, y, x_rel[1], c), at(z, y, x_rel[3], c)]
+    greeted += [at(z, y, x_rel[r], c) for r in range(1, NX)]
     greeted += [at(z, lax.rem(y + d, NY), x, c) for d in range(1, NY)]
     for device in greeted:
         pl.semaphore_signal(barrier, inc=1, device_id=device, device_id_type=MESH)
@@ -191,68 +193,73 @@
     second_to = (x_rel[3], x_rel[1])
 
     def att_first(g):
-        if not ATT:
-            return
-        core_copy[g].wait_recv()
+        arrived(core_in.at[g], core_recv.at[g])
         for h in range(2):
-            cols = pl.ds(h * HALF, HALF)
+            rows, cols = pl.ds(h * HALF, HALF), pl.ds(0, MAIN)
             for j in (2, 3):
                 at_x = x_rel[slots[h][j]]
                 for i in range(2):
-                    send_a[g, h, j - 2, i] = grad[2 * g + i, at_x, c, :, cols] + core_in[g, i, at_x, :, cols]
-            remote(
-                send_a.at[g, h], recv_a.at[g, h], a_send.at[0], a_recv.at[g], at(z, y, first_to[h], c)
-            )
+                    send_a[g, h, j - 2, i] = grad[2 * g + i, at_x, c, rows, cols] + core_in[g, i, at_x, rows, cols]
+            remote(send_a.at[g, h], recv_a.at[g, h], a_send.at[0], a_recv.at[g], at(z, y, first_to[h], c))
+        for i in (2 * g, 2 * g + 1):
+            d, cols = Y_ORDER[i], pl.ds(MAIN, COLS - MAIN)
+            for at_x in range(NX):
+                side[d, at_x] = grad[i, at_x, c, :, cols] + core_in[g, i - 2 * g, at_x, :, cols]
+            if d:
+                remote(side.at[d], side_in.at[d - 1], side_send.at[0], side_recv.at[0], at(z, lax.rem(y + d, NY), x, c))
         for h in range(2):
-            cols = pl.ds(h * HALF, HALF)
+            rows, cols = pl.ds(h * HALF, HALF), pl.ds(0, MAIN)
             for j in (0, 1):
                 at_x = x_rel[slots[h][j]]
                 for i in range(2):
-                    keep[g, h, j, i] = grad[2 * g + i, at_x, c, :, cols] + core_in[g, i, at_x, :, cols]
+                    keep[g, h, j, i] = grad[2 * g + i, at_x, c, rows, cols] + core_in[g, i, at_x, rows, cols]
 
     def att_second(g):
-        if not ATT:
-            return
         arrived(recv_a.at[g], a_recv.at[g])
         for h in range(2):
             send_b[g, h] = keep[g, h, 1] + recv_a[g, h, 1]
-            remote(
-                send_b.at[g, h], recv_b.at[g, h], b_send.at[0], b_recv.at[g], at(z, y, second_to[h], c)
-            )
+            remote(send_b.at[g, h], recv_b.at[g, h], b_send.at[0], b_recv.at[g], at(z, y, second_to[h], c))
+        for h in range(2):
             keep_b[g, h] = keep[g, h, 0] + recv_a[g, h, 0]
 
     def att_third(g):
-        if not ATT:
-            return
         arrived(recv_b.at[g], b_recv.at[g])
         for h in range(2):
             for i in range(2):
-                y_out[2 * g + i, :, pl.ds(h * HALF, HALF)] = keep_b[g, h, i] + recv_b[g, h, i]
+                y_out[2 * g + i, pl.ds(h * HALF, HALF)] = keep_b[g, h, i] + recv_b[g, h, i]
         for i in (2 * g, 2 * g + 1):
             d = Y_ORDER[i]
             if d:
-                remote(
-                    y_out.at[i], y_in.at[d - 1], y_send.at[0], y_recv.at[0], at(z, lax.rem(y + d, NY), x, c)
-                )
-
-    def att_last():
-        if not ATT:
-            return
+                remote(y_out.at[i], y_in.at[d - 1], y_send.at[0], y_recv.at[0], at(z, lax.rem(y + d, NY), x, c))
+
+    def att_cross(g):
+        arrived(side_in, side_recv.at[0])
+        total = side[0]
+        for d in range(1, NY):
+            total = total + side_in[d - 1]
+        cross[...] = total
+        for r in (2, 1, 3):
+            remote(cross.at[x_rel[r]], cross_in.at[r - 1], cross_send.at[0], cross_recv.at[0], at(z, y, x_rel[r], c))
+
+    def att_last(g):
+        arrived(cross_in, cross_recv.at[0])
+        total = cross[x]
+        for r in range(1, NX):
+            total = total + cross_in[r - 1]
+        att_ref[:, pl.ds(MAIN, COLS - MAIN)] = total
+        squares.append(squares_of(total))
         arrived(y_in, y_recv.at[0])
         total = y_out[Y_ORDER.index(0)]
-        for d in Y_ORDER:
-            if d:
-                total = total + y_in[d - 1]
-        att_ref[...] = total
+        for d in range(1, NY):
+            total = total + y_in[d - 1]
+        att_ref[:, pl.ds(0, MAIN)] = total
+        squares.append(squares_of(total))
         pltpu.make_async_copy(att_ref, att_hbm, out_sem.at[1]).start()
-        squares.append(squares_of(total))
-
-    work = {"second": att_second, "third": att_third, "last": lambda g: att_last()}
-
+
+    work = {"second": att_second, "third": att_third, "cross": att_cross, "last": att_last}
+
+    exp_piece(0)
     pl.semaphore_wait(barrier, len(greeted))
-    att_group(0)
-    att_group(1)
-    exp_piece(0)
     ring_start(0, 0)
     exp_piece(2)
     ring_start(1, 2)
@@ -264,6 +271,8 @@
     ring_start(1, 0)
     ring_start(0, 3)
     ring_start(1, 1)
+    att_group(0)
+    att_group(1)
     att_group(2)
     att_group(3)
     for g in range(GROUPS):
@@ -292,7 +301,8 @@
         norm_copy(0, norm_c, norm_z.at[0], at(z, y, x, 1)).start()
 
     for ref, sem in (
-        (ring, ring_send), (core_in, core_send), (send_a, a_send), (send_b, b_send), (y_in, y_send), (exp_ref, out_sem)
+        (ring, ring_send), (core_in, core_send), (send_a, a_send), (send_b, b_send), (y_in, y_send), (exp_ref, out_sem),
+        (side_in, side_send), (cross_in, cross_send),
     ):
         arrived(ref, sem.at[0])
     arrived(att_ref, out_sem.at[1])
@@ -348,14 +358,18 @@
             pltpu.VMEM((len(STEPS), 2, OWN, WIDE), f32),
             pltpu.VMEM((NY, NX, NC, ROWS, COLS), f32),
             pltpu.VMEM((GROUPS, 2, NX, ROWS, COLS), f32),
-            pltpu.VMEM((GROUPS, 2, 2, 2, ROWS, HALF), f32),
-            pltpu.VMEM((GROUPS, 2, 2, 2, ROWS, HALF), f32),
-            pltpu.VMEM((GROUPS, 2, 2, 2, ROWS, HALF), f32),
-            pltpu.VMEM((GROUPS, 2, 2, ROWS, HALF), f32),
-            pltpu.VMEM((GROUPS, 2, 2, ROWS, HALF), f32),
-            pltpu.VMEM((GROUPS, 2, 2, ROWS, HALF), f32),
-            pltpu.VMEM((NY, ROWS, COLS), f32),
-            pltpu.VMEM((NY - 1, ROWS, COLS), f32),
+            pltpu.VMEM((GROUPS, 2, 2, 2, HALF, MAIN), f32),
+            pltpu.VMEM((GROUPS, 2, 2, 2, HALF, MAIN), f32),
+            pltpu.VMEM((GROUPS, 2, 2, 2, HALF, MAIN), f32),
+            pltpu.VMEM((GROUPS, 2, 2, HALF, MAIN), f32),
+            pltpu.VMEM((GROUPS, 2, 2, HALF, MAIN), f32),
+            pltpu.VMEM((GROUPS, 2, 2, HALF, MAIN), f32),
+            pltpu.VMEM((NY, ROWS, MAIN), f32),
+            pltpu.VMEM((NY - 1, ROWS, MAIN), f32),
+            pltpu.VMEM((NY, NX, ROWS, COLS - MAIN), f32),
+            pltpu.VMEM((NY - 1, NX, ROWS, COLS - MAIN), f32),
+            pltpu.VMEM((NX, ROWS, COLS - MAIN), f32),
+            pltpu.VMEM((NX - 1, ROWS, COLS - MAIN), f32),
             pltpu.VMEM((1, 128), f32),
             pltpu.VMEM((NZ * NC, 1, 128), f32),
             pltpu.VMEM((NX * NY, 1, 128), f32),
@@ -368,6 +382,10 @@
             dma((GROUPS,)),
             dma((1,)),
             dma((GROUPS,)),
+            dma((1,)),
+            dma((1,)),
+            dma((1,)),
+            dma((1,)),
             dma((1,)),
             dma((1,)),
             dma((2,)),

time: 45.8 us -> 44.7 us (0.976)
  Pallas kernels: 44.2 us -> 43 us
    pallas_call x1, Pallas kernels: 42 us -> 40.9 us  [grads(): pl.pallas_call(grads_kernel, out_shape=tuple((jax.ShapeDtypeStruct(shape,...]
where the time goes in v5:
time: 44.7 us; the launch traced here: 44.4 us
  Pallas kernels  43 us (96%)
  between operations  1.35 us (3%)
    pallas_call x1, Pallas kernels, grads(): pl.pallas_call(grads_kernel, out_shape=tuple((jax.ShapeDtypeStruct(shape,...  40.9 us
    pallas_call x1, Pallas kernels, update(): pl.pallas_call(update_kernel, out_shape=tuple((jax.ShapeDtypeStruct(a.sha...  2.11 us

profile of v5, /device:TPU:1, one launch (start us, length us, event | category | flops | bytes accessed | tf_op | source)
XLA Modules:
  0.0 44.4 jit_solution(10300634001253257193)
XLA Ops:
  0.6 0.0 copy-start.2
  0.6 0.0 copy-start.1
  0.7 0.0 copy-start
  1.3 40.9 %grads.1 = (f32[24,2048]{1,0:T(8,128)}, f32[16,512]{1,0:T(8,128)S(1)}, f32[1,128]{1,0:T(1,128)S(1)}) custom-call(bf16[192,384]{1,0:T(8,128)(2,1)} %bitcast.1, bf16[384,2048]{1,0:T(8,128)(2,1)} %cot_hbm.1, bf16[384,1024]{1,0:T(8,128)(2,1)} %kv_hbm.1, bf16[384,512]{1,0:T(8,128)(2,1)} %x_hbm.1, s32[1,1]{1,0:T(1,128)S(6)} %copy.17.count_hbm), custom_call_target="tpu_custom_call" | custom-call | tf_op jit(solution)/shard_map/grads/pallas_call | solution.py:343
  42.3 0.0 copy-done.2
  42.3 0.0 copy-done.1
  42.3 0.0 copy-done
  42.3 2.1 %update.1 = (f32[16,512]{1,0:T(8,128)}, f32[16,512]{1,0:T(8,128)}, f32[16,512]{1,0:T(8,128)}, f32[24,2048]{1,0:T(8,128)}, f32[24,2048]{1,0:T(8,128)}, /*index=5*/f32[24,2048]{1,0:T(8,128)}) custom-call(f32[1,128]{1,0:T(1,128)S(1)} %get-tuple-element.9.norm_hbm, f32[16,512]{1,0:T(8,128)S(1)} %copy-done, f32[16,512]{1,0:T(8,128)S(1)} %copy-done.1, ...), custom_call_target="tpu_custom_call" | custom-call | tf_op jit(solution)/shard_map/update/pallas_call | solution.py:456
Async XLA Ops:
  0.6 41.6 %copy-start.2 = (f32[16,512]{1,0:T(8,128)S(1)}, f32[16,512]{1,0:T(8,128)}, u32[]{:S(2)}) copy-start(f32[16,512]{1,0:T(8,128)} %refs_2_.1) | copy-start | bytes 98308
  0.6 41.6 %copy-start.1 = (f32[16,512]{1,0:T(8,128)S(1)}, f32[16,512]{1,0:T(8,128)}, u32[]{:S(2)}) copy-start(f32[16,512]{1,0:T(8,128)} %refs_1_.1) | copy-start | bytes 98308
  0.7 41.6 %copy-start = (f32[16,512]{1,0:T(8,128)S(1)}, f32[16,512]{1,0:T(8,128)}, u32[]{:S(2)}) copy-start(f32[16,512]{1,0:T(8,128)} %refs_0_.1) | copy-start | bytes 98308

commit v6 on v5

--- a/solution.py
+++ b/solution.py
@@ -99,7 +99,7 @@
     loads.append(pltpu.make_async_copy(kv_hbm, kv, load_sem.at[2 + PIECES]))
     count_load = pltpu.make_async_copy(count_hbm, count_ref, load_sem.at[3 + PIECES])
     count_load.start()
-    for n in (1 + PIECES, 2 + PIECES, *range(1 + PIECES)):
+    for n in (0, 1, 1 + SPLIT, 2, 2 + SPLIT, 1 + PIECES, 2 + PIECES):
         loads[n].start()
 
     def squares_of(value):
@@ -321,10 +321,11 @@
         norm_p[0] = jnp.sum(norm_z[...], axis=0)
         plane = [(dy, dx) for dy in range(NY) for dx in range(NX) if dy or dx]
         plane.sort(key=lambda e: -min(e[0], NY - e[0]) - min(e[1], NX - e[1]))
-        for core in range(NC):
-            for dy, dx in plane if core else plane + [(0, 0)]:
+        for dy, dx in plane:
+            for core in range(NC):
                 device = at(z, lax.rem(y + dy, NY), lax.rem(x + dx, NX), core)
                 norm_copy(1, norm_p.at[0], norm_p.at[dy * NX + dx], device).start()
+        norm_copy(1, norm_p.at[0], norm_p.at[0], at(z, y, x, 0)).start()
         sent = norm_z.at[pl.ds(0, NZ - 1)]
         pltpu.make_async_copy(sent, sent, norm_send.at[0]).wait()
         others = norm_p.at[pl.ds(1, NX * NY - 1)]

time: 44.7 us -> 44.5 us (level)
  no operation moved by 1% of the time
where the time goes in v6:
time: 44.5 us; the launch traced here: 44.2 us
  Pallas kernels  42.9 us (96%)
  between operations  1.35 us (3%)
    pallas_call x1, Pallas kernels, grads(): pl.pallas_call(grads_kernel, out_shape=tuple((jax.ShapeDtypeStruct(shape,...  40.8 us
    pallas_call x1, Pallas kernels, update(): pl.pallas_call(update_kernel, out_shape=tuple((jax.ShapeDtypeStruct(a.sha...  2.11 us

profile of v6, /device:TPU:1, one launch (start us, length us, event | category | flops | bytes accessed | tf_op | source)
XLA Modules:
  0.0 44.2 jit_solution(787192680557395255)
XLA Ops:
  0.6 0.0 copy-start.2
  0.6 0.0 copy-start.1
  0.7 0.0 copy-start
  1.3 40.8 %grads.1 = (f32[24,2048]{1,0:T(8,128)}, f32[16,512]{1,0:T(8,128)S(1)}, f32[1,128]{1,0:T(1,128)S(1)}) custom-call(bf16[192,384]{1,0:T(8,128)(2,1)} %bitcast.1, bf16[384,2048]{1,0:T(8,128)(2,1)} %cot_hbm.1, bf16[384,1024]{1,0:T(8,128)(2,1)} %kv_hbm.1, bf16[384,512]{1,0:T(8,128)(2,1)} %x_hbm.1, s32[1,1]{1,0:T(1,128)S(6)} %copy.17.count_hbm), custom_call_target="tpu_custom_call" | custom-call | tf_op jit(solution)/shard_map/grads/pallas_call | solution.py:344
  42.1 0.0 copy-done.2
  42.1 0.0 copy-done.1
  42.1 0.0 copy-done
  42.1 2.1 %update.1 = (f32[16,512]{1,0:T(8,128)}, f32[16,512]{1,0:T(8,128)}, f32[16,512]{1,0:T(8,128)}, f32[24,2048]{1,0:T(8,128)}, f32[24,2048]{1,0:T(8,128)}, /*index=5*/f32[24,2048]{1,0:T(8,128)}) custom-call(f32[1,128]{1,0:T(1,128)S(1)} %get-tuple-element.9.norm_hbm, f32[16,512]{1,0:T(8,128)S(1)} %copy-done, f32[16,512]{1,0:T(8,128)S(1)} %copy-done.1, ...), custom_call_target="tpu_custom_call" | custom-call | tf_op jit(solution)/shard_map/update/pallas_call | solution.py:457
Async XLA Ops:
  0.6 41.5 %copy-start.2 = (f32[16,512]{1,0:T(8,128)S(1)}, f32[16,512]{1,0:T(8,128)}, u32[]{:S(2)}) copy-start(f32[16,512]{1,0:T(8,128)} %refs_2_.1) | copy-start | bytes 98308
  0.6 41.5 %copy-start.1 = (f32[16,512]{1,0:T(8,128)S(1)}, f32[16,512]{1,0:T(8,128)}, u32[]{:S(2)}) copy-start(f32[16,512]{1,0:T(8,128)} %refs_1_.1) | copy-start | bytes 98308
  0.7 41.5 %copy-start = (f32[16,512]{1,0:T(8,128)S(1)}, f32[16,512]{1,0:T(8,128)}, u32[]{:S(2)}) copy-start(f32[16,512]{1,0:T(8,128)} %refs_0_.1) | copy-start | bytes 98308

commit v7 on v6

--- a/solution.py
+++ b/solution.py
@@ -293,12 +293,15 @@
             device_id=device, device_id_type=MESH,
         )
 
-    for d in (4, 3, 5, 2, 6, 1, 7):
-        norm_copy(0, norm_c, norm_z.at[d * NC + c], at(lax.rem(z + d, NZ), y, x, 1)).start()
+    plane = [(dy, dx) for dy in range(NY) for dx in range(NX) if dy or dx]
+    plane.sort(key=lambda e: -min(e[0], NY - e[0]) - min(e[1], NX - e[1]))
+    for dy, dx in plane:
+        device = at(z, lax.rem(y + dy, NY), lax.rem(x + dx, NX), 1)
+        norm_copy(0, norm_c, norm_p.at[(dy * NX + dx) * NC + c], device).start()
 
     @pl.when(c == 0)
     def _():
-        norm_copy(0, norm_c, norm_z.at[0], at(z, y, x, 1)).start()
+        norm_copy(0, norm_c, norm_p.at[0], at(z, y, x, 1)).start()
 
     for ref, sem in (
         (ring, ring_send), (core_in, core_send), (send_a, a_send), (send_b, b_send), (y_in, y_send), (exp_ref, out_sem),
@@ -309,31 +312,25 @@
 
     @pl.when(c == 0)
     def _():
-        sent = norm_z.at[pl.ds(0, NZ)]
-        pltpu.make_async_copy(sent, sent, norm_send.at[0]).wait()
-        pltpu.make_async_copy(norm_p, norm_p, norm_recv.at[1]).wait()
+        arrived(norm_p.at[pl.ds(0, NX * NY)], norm_send.at[0])
+        arrived(norm_z, norm_recv.at[1])
 
     @pl.when(c == 1)
     def _():
-        norm_z[1] = norm_c[...]
-        others = norm_z.at[pl.ds(0, NZ * NC - 1)]
-        pltpu.make_async_copy(others, others, norm_recv.at[0]).wait()
-        norm_p[0] = jnp.sum(norm_z[...], axis=0)
-        plane = [(dy, dx) for dy in range(NY) for dx in range(NX) if dy or dx]
-        plane.sort(key=lambda e: -min(e[0], NY - e[0]) - min(e[1], NX - e[1]))
-        for dy, dx in plane:
+        norm_p[1] = norm_c[...]
+        arrived(norm_p.at[pl.ds(0, NX * NY * NC - 1)], norm_recv.at[0])
+        norm_z[0] = jnp.sum(norm_p[...], axis=0)
+        for d in (4, 3, 5, 2, 6, 1, 7):
             for core in range(NC):
-                device = at(z, lax.rem(y + dy, NY), lax.rem(x + dx, NX), core)
-                norm_copy(1, norm_p.at[0], norm_p.at[dy * NX + dx], device).start()
-        norm_copy(1, norm_p.at[0], norm_p.at[0], at(z, y, x, 0)).start()
-        sent = norm_z.at[pl.ds(0, NZ - 1)]
-        pltpu.make_async_copy(sent, sent, norm_send.at[0]).wait()
-        others = norm_p.at[pl.ds(1, NX * NY - 1)]
-        pltpu.make_async_copy(others, others, norm_recv.at[1]).wait()
-        for sent in (norm_p, others):
-            pltpu.make_async_copy(sent, sent, norm_send.at[1]).wait()
-
-    norm_ref[...] = jnp.sum(norm_p[...], axis=0)
+                norm_copy(1, norm_z.at[0], norm_z.at[d], at(lax.rem(z + d, NZ), y, x, core)).start()
+        norm_copy(1, norm_z.at[0], norm_z.at[0], at(z, y, x, 0)).start()
+        arrived(norm_p.at[pl.ds(0, NX * NY - 1)], norm_send.at[0])
+        others = norm_z.at[pl.ds(1, NZ - 1)]
+        arrived(others, norm_recv.at[1])
+        arrived(norm_z, norm_send.at[1])
+        arrived(others, norm_send.at[1])
+
+    norm_ref[...] = jnp.sum(norm_z[...], axis=0)
 
 
 def grads(hidden, cot, kv, xin, counts):
@@ -372,8 +369,8 @@
             pltpu.VMEM((NX, ROWS, COLS - MAIN), f32),
             pltpu.VMEM((NX - 1, ROWS, COLS - MAIN), f32),
             pltpu.VMEM((1, 128), f32),
-            pltpu.VMEM((NZ * NC, 1, 128), f32),
-            pltpu.VMEM((NX * NY, 1, 128), f32),
+            pltpu.VMEM((NZ, 1, 128), f32),
+            pltpu.VMEM((NX * NY * NC, 1, 128), f32),
             dma((4 + PIECES,)),
             dma((1,)),
             dma((len(STEPS),)),
@@ -408,12 +405,12 @@
     norm, att, exp, new_att, new_exp, load_sem, store_sem = refs[14:]
     wide = DW // BLOCKS
     cols = [pl.ds(n * wide, wide) for n in range(BLOCKS)]
+    for n in range(BLOCKS):
+        for i, a in enumerate(exp_in):
+            pltpu.make_async_copy(a.at[:, cols[n]], exp.at[i, :, cols[n]], load_sem.at[2 + n]).start()
     pltpu.make_async_copy(norm_hbm, norm, load_sem.at[0]).start()
     for i, a in enumerate(att_in):
         pltpu.make_async_copy(a, att.at[i], load_sem.at[1]).start()
-    for n in range(BLOCKS):
-        for i, a in enumerate(exp_in):
-            pltpu.make_async_copy(a.at[:, cols[n]], exp.at[i, :, cols[n]], load_sem.at[2 + n]).start()
 
     def arrived(ref, sem):
         pltpu.make_async_copy(ref, ref, sem).wait()

time: 44.5 us -> 44.4 us (level)
  no operation moved by 1% of the time
where the time goes in v7:
time: 44.4 us; the launch traced here: 44.1 us
  Pallas kernels  42.7 us (96%)
  between operations  1.35 us (3%)
    pallas_call x1, Pallas kernels, grads(): pl.pallas_call(grads_kernel, out_shape=tuple((jax.ShapeDtypeStruct(shape,...  40.8 us
    pallas_call x1, Pallas kernels, update(): pl.pallas_call(update_kernel, out_shape=tuple((jax.ShapeDtypeStruct(a.sha...  1.93 us

profile of v7, /device:TPU:1, one launch (start us, length us, event | category | flops | bytes accessed | tf_op | source)
XLA Modules:
  0.0 44.1 jit_solution(6772706891630582952)
XLA Ops:
  0.6 0.0 copy-start.2
  0.6 0.0 copy-start.1
  0.7 0.0 copy-start
  1.3 40.8 %grads.1 = (f32[24,2048]{1,0:T(8,128)}, f32[16,512]{1,0:T(8,128)S(1)}, f32[1,128]{1,0:T(1,128)S(1)}) custom-call(bf16[192,384]{1,0:T(8,128)(2,1)} %bitcast.1, bf16[384,2048]{1,0:T(8,128)(2,1)} %cot_hbm.1, bf16[384,1024]{1,0:T(8,128)(2,1)} %kv_hbm.1, bf16[384,512]{1,0:T(8,128)(2,1)} %x_hbm.1, s32[1,1]{1,0:T(1,128)S(6)} %copy.17.count_hbm), custom_call_target="tpu_custom_call" | custom-call | tf_op jit(solution)/shard_map/grads/pallas_call | solution.py:341
  42.1 0.0 copy-done.2
  42.2 0.0 copy-done.1
  42.2 0.0 copy-done
  42.2 1.9 %update.1 = (f32[16,512]{1,0:T(8,128)}, f32[16,512]{1,0:T(8,128)}, f32[16,512]{1,0:T(8,128)}, f32[24,2048]{1,0:T(8,128)}, f32[24,2048]{1,0:T(8,128)}, /*index=5*/f32[24,2048]{1,0:T(8,128)}) custom-call(f32[1,128]{1,0:T(1,128)S(1)} %get-tuple-element.9.norm_hbm, f32[16,512]{1,0:T(8,128)S(1)} %copy-done, f32[16,512]{1,0:T(8,128)S(1)} %copy-done.1, ...), custom_call_target="tpu_custom_call" | custom-call | tf_op jit(solution)/shard_map/update/pallas_call | solution.py:454
Async XLA Ops:
  0.6 41.5 %copy-start.2 = (f32[16,512]{1,0:T(8,128)S(1)}, f32[16,512]{1,0:T(8,128)}, u32[]{:S(2)}) copy-start(f32[16,512]{1,0:T(8,128)} %refs_2_.1) | copy-start | bytes 98308
  0.6 41.5 %copy-start.1 = (f32[16,512]{1,0:T(8,128)S(1)}, f32[16,512]{1,0:T(8,128)}, u32[]{:S(2)}) copy-start(f32[16,512]{1,0:T(8,128)} %refs_1_.1) | copy-start | bytes 98308
  0.7 41.5 %copy-start = (f32[16,512]{1,0:T(8,128)S(1)}, f32[16,512]{1,0:T(8,128)}, u32[]{:S(2)}) copy-start(f32[16,512]{1,0:T(8,128)} %refs_0_.1) | copy-start | bytes 98308
